TPU v7x, 32 devices: a whole 2x2x4 slice. The times are simulated.
32 devices in a mesh: parts: 2 (over y), seq: 16 (over z, x, core).
Axes of the slice: x: 2, y: 2, z: 4, core: 2. Of those that a mesh axis runs over, the one named last changes fastest.
Arguments:
- queries: bfloat16 [32, 8192], P(('parts', 'seq')), parts along dimension 0, may hold values from -140 to 140
- new_keys: bfloat16 [32, 1024], P(('parts', 'seq')), parts along dimension 0, may hold values from -7 to 7
- new_values: bfloat16 [32, 1024], P(('parts', 'seq')), parts along dimension 0, may hold values from -6 to 6
- doc_keys: bfloat16 [32768, 1024], P(('parts', 'seq')), parts along dimension 0, may hold values from -6 to 6
- doc_values: bfloat16 [32768, 1024], P(('parts', 'seq')), parts along dimension 0, may hold values from -6 to 6
- suffix_keys: bfloat16 [32768, 1024], P(('parts', 'seq')), parts along dimension 0, may hold values from -6 to 6
- suffix_values: bfloat16 [32768, 1024], P(('parts', 'seq')), parts along dimension 0, may hold values from -6 to 6
- keep_lists: int32 [32, 32], P(('parts', 'seq')), parts along dimension 0, may hold values from 0 to 127, as said below
- suffix_lengths: int32 [16], P('parts'), parts along dimension 0, may hold values from 1 to 2048
Outputs:
- attended: bfloat16 [32, 8192], P(('parts', 'seq')), parts along dimension 0
There are 2 independent parts, one for each index of `parts`. A program takes and returns all parts, laid end to end along the dimension named above; each array names one. Nothing has to cross between parts.
Inputs may be any that keep to these rules, and one draw needn't show every extreme that they name: Row r's list (rows 2r and 2r+1 of keep_lists) names 64 different blocks of 0 to 127.
All inputs are finite; a program needn't handle non-finite values.
Results may differ from a plain program's by a relative error of at most 0.007.
Values may be sent and summed in bfloat16 or wider, within the bound.
A program may use at most 128 MiB of HBM per device.

v0:
```python
import jax
import jax.numpy as jnp
from jax import lax
from jax.sharding import PartitionSpec as P

HEADS = 64
KVH = 8
HD = 128
BLOCK = 128


NEG_BIG = -1e30


def merge_terms(first, second):
    ceiling = jnp.maximum(first[0], second[0])
    left_scale = jnp.exp(first[0] - ceiling)
    right_scale = jnp.exp(second[0] - ceiling)
    return (
        ceiling,
        left_scale * first[1] + right_scale * second[1],
        left_scale[..., None] * first[2] + right_scale[..., None] * second[2],
    )


def block_terms(scores, live_keys, value_rows, form):
    masked = jnp.where(live_keys, scores, NEG_BIG)
    block_max = jnp.max(masked, axis=-1)
    weights = jnp.where(live_keys, jnp.exp(scores - block_max[..., None]), 0.0)
    block_sum = jnp.sum(weights, axis=-1)
    block_out = jnp.einsum(
        form, weights.astype(jnp.bfloat16), value_rows, preferred_element_type=jnp.float32
    )
    global_maximum = jnp.max(block_max, axis=-1)
    factor = jnp.exp(block_max - global_maximum[..., None])
    return (
        global_maximum,
        jnp.sum(factor * block_sum, axis=-1),
        jnp.sum(factor[..., None] * block_out, axis=-2),
    )


def per_device(
    queries,
    new_keys,
    new_values,
    doc_keys,
    doc_values,
    suffix_keys,
    suffix_values,
    keep_lists,
    suffix_lengths,
):
    groups = HEADS // KVH
    factor_scale = HD ** (-0.5)
    devices = lax.axis_size("seq")
    my_index = lax.axis_index("seq")
    row_id = my_index // 2
    parity = my_index % 2
    blocks_here = doc_keys.shape[0] // BLOCK
    gathered = lax.all_gather(queries, "seq", axis=0, tiled=True)
    every_list = lax.all_gather(keep_lists, "seq", axis=0, tiled=True)
    local_ids = every_list.reshape(devices // 2, -1) - my_index * blocks_here
    block_range = jnp.arange(blocks_here, dtype=jnp.int32)
    row_hits = jnp.any(local_ids[:, :, None] == block_range[None, None, :], axis=1)
    token_mask = jnp.repeat(row_hits, 2, axis=0)
    q_heads = gathered.reshape(devices, KVH, groups, HD).transpose(1, 0, 2, 3)
    key_heads = doc_keys.reshape(blocks_here, BLOCK, KVH, HD).transpose(2, 0, 1, 3)
    value_heads = doc_values.reshape(blocks_here, BLOCK, KVH, HD).transpose(2, 0, 1, 3)

    def doc_head(head_item):
        q_part, key_part, value_part = head_item
        scores = (
            jnp.einsum("tgd,bjd->tgbj", q_part, key_part, preferred_element_type=jnp.float32)
            * factor_scale
        )
        return block_terms(scores, token_mask[:, None, :, None], value_part, "tgbj,bjd->tgbd")

    doc_max, doc_sum, doc_out = lax.map(doc_head, (q_heads, key_heads, value_heads))
    doc_partial = (
        doc_max.transpose(1, 0, 2).reshape(devices, HEADS),
        doc_sum.transpose(1, 0, 2).reshape(devices, HEADS),
        doc_out.transpose(1, 0, 2, 3).reshape(devices, HEADS, HD),
    )
    q_rows = lax.dynamic_slice_in_dim(gathered, 2 * row_id, 2, 0).reshape(2, KVH, groups, HD)
    suffix_here = suffix_keys.shape[0]
    suffix_blocks = suffix_here // BLOCK
    keys_suf = suffix_keys.reshape(suffix_blocks, BLOCK, KVH, HD)
    values_suf = suffix_values.reshape(suffix_blocks, BLOCK, KVH, HD)
    scores = (
        jnp.einsum("tkgd,bjkd->tkgbj", q_rows, keys_suf, preferred_element_type=jnp.float32)
        * factor_scale
    )
    position = parity * suffix_here + jnp.arange(suffix_here, dtype=jnp.int32).reshape(
        suffix_blocks, BLOCK
    )
    live_keys = position < suffix_lengths[row_id]
    row_partial = block_terms(scores, live_keys, values_suf, "tkgbj,bjkd->tkgbd")
    own_scores = (
        jnp.einsum(
            "tkgd,kd->tkg", q_rows, new_keys.reshape(KVH, HD), preferred_element_type=jnp.float32
        )
        * factor_scale
    )
    visible = jnp.broadcast_to(
        (jnp.arange(2, dtype=jnp.int32) >= parity)[:, None, None], own_scores.shape
    )
    own_values = jnp.broadcast_to(
        new_values.reshape(KVH, HD).astype(jnp.float32)[None, :, None, :], (2, KVH, groups, HD)
    )
    own_partial = (
        jnp.where(visible, own_scores, NEG_BIG),
        visible.astype(jnp.float32),
        jnp.where(visible[..., None], own_values, 0.0),
    )
    row_partial = merge_terms(row_partial, own_partial)
    placed = (
        lax.dynamic_update_slice(
            jnp.full((devices, HEADS), NEG_BIG, jnp.float32),
            row_partial[0].reshape(2, HEADS),
            (2 * row_id, 0),
        ),
        lax.dynamic_update_slice(
            jnp.zeros((devices, HEADS), jnp.float32),
            row_partial[1].reshape(2, HEADS),
            (2 * row_id, 0),
        ),
        lax.dynamic_update_slice(
            jnp.zeros((devices, HEADS, HD), jnp.float32),
            row_partial[2].reshape(2, HEADS, HD),
            (2 * row_id, 0, 0),
        ),
    )
    span_max, span_sum, span_out = merge_terms(doc_partial, placed)
    units = (span_out / jnp.maximum(span_sum, 1.0)[..., None]).astype(jnp.bfloat16)
    parts_max, parts_sum = (
        lax.all_to_all(span_max[:, None, :], "seq", split_axis=0, concat_axis=1, tiled=True),
        lax.all_to_all(span_sum[:, None, :], "seq", split_axis=0, concat_axis=1, tiled=True),
    )
    parts_unit = lax.all_to_all(
        units.reshape(devices, 1, HEADS * HD), "seq", split_axis=0, concat_axis=1, tiled=True
    )
    ceiling = jnp.max(parts_max, axis=1)
    weight = jnp.exp(parts_max - ceiling[:, None, :]) * parts_sum
    total_sum = jnp.sum(weight, axis=1)
    total_out = jnp.sum(
        weight[..., None] * parts_unit.reshape(1, devices, HEADS, HD).astype(jnp.float32), axis=1
    )
    return (total_out / total_sum[..., None]).reshape(1, HEADS * HD).astype(jnp.bfloat16)


def solution(mesh):
    in_specs = (
        P(("parts", "seq"), None),
        P(("parts", "seq"), None),
        P(("parts", "seq"), None),
        P(("parts", "seq"), None),
        P(("parts", "seq"), None),
        P(("parts", "seq"), None),
        P(("parts", "seq"), None),
        P(("parts", "seq"), None),
        P("parts"),
    )
    out_specs = P(("parts", "seq"), None)
    return jax.shard_map(
        per_device, mesh=mesh, in_specs=in_specs, out_specs=out_specs, check_vma=False
    )
```

profile of v0, /device:TPU:0, one launch (start us, length us, event | category | flops | bytes accessed | tf_op | source)
XLA Modules:
  0.0 115.0 jit_solution(774386942064762164)
XLA Ops:
  0.0 24.8 %all-gather.1 = bf16[16,1,8192]{2,1,0:T(2,128)(2,1)S(1)} all-gather(bf16[1,1,8192]{2,1,0:T(2,128)(2,1)} %bitcast.210), channel_id=1, replica_groups=mesh['parts'=2,'seq'=16] {'seq'}, dimensions={0}, use_global_device_ids=true | all-gather | bytes 278528 | tf_op jit(solution)/shard_map/all_gather | solution.py:61
  24.8 2.2 %copy.160 = bf16[128,8,8,128]{3,2,1,0:T(8,128)(2,1)S(1)} copy(bf16[128,8,8,128]{3,1,2,0:T(8,128)(2,1)} %bitcast.191) | data formatting | bytes 4194304
  28.4 0.7 add_compare_fusion
  29.3 0.8 select_reduce_fusion.2
  30.1 0.9 fusion.38
  31.1 0.7 fusion.54
  32.0 17.3 %all-gather = s32[16,1,32]{2,1,0:T(1,128)S(1)} all-gather(s32[1,1,32]{2,1,0:T(1,128)S(1)} %bitcast.212), channel_id=1, replica_groups=mesh['parts'=2,'seq'=16] {'seq'}, dimensions={0}, use_global_device_ids=true | all-gather | bytes 2176 | tf_op jit(solution)/shard_map/all_gather | solution.py:62
  49.7 1.6 %reduce.8 = bf16[16,8192]{1,0:T(8,128)(2,1)S(1)} reduce(bf16[16,1,8192]{2,1,0:T(2,128)(2,1)S(1)} %all-gather.1, bf16[]{:T(256)} %constant.83), dimensions={1}, to_apply=%all-gather.1.reduce_sub_computation | reduce | bytes 524290 | tf_op jit(solution)/shard_map/all_gather | solution.py:61
  52.7 1.1 copy-done.2
  54.5 1.9 %copy.116 = bf16[8,8,128,128]{3,2,1,0:T(8,128)(2,1)} copy(bf16[8,8,128,128]{3,0,2,1:T(8,128)(2,1)S(1)} %bitcast_bitcast_fusion.2) | data formatting | bytes 4194304
  56.4 20.4 %while.15 = (s32[]{:T(128)}, f32[8,16,8]{1,2,0:T(8,128)S(1)}, f32[8,16,8]{1,2,0:T(8,128)S(1)}, f32[8,16,8,128]{3,2,0,1:T(8,128)S(1)}, bf16[8,16,8,128]{3,2,0,1:T...) while((s32[]{:T(128)}, f32[8,16,8]{1,2,0:T(8,128)S(1)}, ...), condition=%wide.region_7.8_spmd.clone, body=%wide.region_1.7_spmd.clone.sunk | while | flops 68535040 | bytes 2387621 | solution.py:79
  57.5 1.3 %fusion.67 = f32[16,8,128]{2,0,1:T(8,128)S(1)} fusion(bf16[16,8,8,128]{3,1,2,0:T(8,128)(2,1)S(1)} %get-tuple-element.219, bf16[8,8,128,128]{3,2,1,0:T(8,128)(2,1)} %get-tuple-element.245, s32[]{:T(128)} %get-tuple-element.230, f32[16,8,8]{0,1,2:T(8,128)S(1)} %copy.220), kind=kOutput, calls=%fused_computation.4.clone.1 | convolution fusion | flops 33800192 | bytes 594432 | tf_op jit(solution)/shard_map/while/body/eval_jaxpr/tgbj,bjd->tgbd/dot_general | solution.py:31
  60.1 1.3 %fusion.67 = f32[16,8,128]{2,0,1:T(8,128)S(1)} fusion(bf16[16,8,8,128]{3,1,2,0:T(8,128)(2,1)S(1)} %get-tuple-element.219, bf16[8,8,128,128]{3,2,1,0:T(8,128)(2,1)} %get-tuple-element.245, s32[]{:T(128)} %get-tuple-element.230, f32[16,8,8]{0,1,2:T(8,128)S(1)} %copy.220), kind=kOutput, calls=%fused_computation.4.clone.1 | convolution fusion | flops 33800192 | bytes 594432 | tf_op jit(solution)/shard_map/while/body/eval_jaxpr/tgbj,bjd->tgbd/dot_general | solution.py:31
  62.6 1.3 %fusion.67 = f32[16,8,128]{2,0,1:T(8,128)S(1)} fusion(bf16[16,8,8,128]{3,1,2,0:T(8,128)(2,1)S(1)} %get-tuple-element.219, bf16[8,8,128,128]{3,2,1,0:T(8,128)(2,1)} %get-tuple-element.245, s32[]{:T(128)} %get-tuple-element.230, f32[16,8,8]{0,1,2:T(8,128)S(1)} %copy.220), kind=kOutput, calls=%fused_computation.4.clone.1 | convolution fusion | flops 33800192 | bytes 594432 | tf_op jit(solution)/shard_map/while/body/eval_jaxpr/tgbj,bjd->tgbd/dot_general | solution.py:31
  65.2 1.3 %fusion.67 = f32[16,8,128]{2,0,1:T(8,128)S(1)} fusion(bf16[16,8,8,128]{3,1,2,0:T(8,128)(2,1)S(1)} %get-tuple-element.219, bf16[8,8,128,128]{3,2,1,0:T(8,128)(2,1)} %get-tuple-element.245, s32[]{:T(128)} %get-tuple-element.230, f32[16,8,8]{0,1,2:T(8,128)S(1)} %copy.220), kind=kOutput, calls=%fused_computation.4.clone.1 | convolution fusion | flops 33800192 | bytes 594432 | tf_op jit(solution)/shard_map/while/body/eval_jaxpr/tgbj,bjd->tgbd/dot_general | solution.py:31
  67.7 1.3 %fusion.67 = f32[16,8,128]{2,0,1:T(8,128)S(1)} fusion(bf16[16,8,8,128]{3,1,2,0:T(8,128)(2,1)S(1)} %get-tuple-element.219, bf16[8,8,128,128]{3,2,1,0:T(8,128)(2,1)} %get-tuple-element.245, s32[]{:T(128)} %get-tuple-element.230, f32[16,8,8]{0,1,2:T(8,128)S(1)} %copy.220), kind=kOutput, calls=%fused_computation.4.clone.1 | convolution fusion | flops 33800192 | bytes 594432 | tf_op jit(solution)/shard_map/while/body/eval_jaxpr/tgbj,bjd->tgbd/dot_general | solution.py:31
  70.2 1.3 %fusion.67 = f32[16,8,128]{2,0,1:T(8,128)S(1)} fusion(bf16[16,8,8,128]{3,1,2,0:T(8,128)(2,1)S(1)} %get-tuple-element.219, bf16[8,8,128,128]{3,2,1,0:T(8,128)(2,1)} %get-tuple-element.245, s32[]{:T(128)} %get-tuple-element.230, f32[16,8,8]{0,1,2:T(8,128)S(1)} %copy.220), kind=kOutput, calls=%fused_computation.4.clone.1 | convolution fusion | flops 33800192 | bytes 594432 | tf_op jit(solution)/shard_map/while/body/eval_jaxpr/tgbj,bjd->tgbd/dot_general | solution.py:31
  72.8 1.3 %fusion.67 = f32[16,8,128]{2,0,1:T(8,128)S(1)} fusion(bf16[16,8,8,128]{3,1,2,0:T(8,128)(2,1)S(1)} %get-tuple-element.219, bf16[8,8,128,128]{3,2,1,0:T(8,128)(2,1)} %get-tuple-element.245, s32[]{:T(128)} %get-tuple-element.230, f32[16,8,8]{0,1,2:T(8,128)S(1)} %copy.220), kind=kOutput, calls=%fused_computation.4.clone.1 | convolution fusion | flops 33800192 | bytes 594432 | tf_op jit(solution)/shard_map/while/body/eval_jaxpr/tgbj,bjd->tgbd/dot_general | solution.py:31
  75.3 1.3 %fusion.67 = f32[16,8,128]{2,0,1:T(8,128)S(1)} fusion(bf16[16,8,8,128]{3,1,2,0:T(8,128)(2,1)S(1)} %get-tuple-element.219, bf16[8,8,128,128]{3,2,1,0:T(8,128)(2,1)} %get-tuple-element.245, s32[]{:T(128)} %get-tuple-element.230, f32[16,8,8]{0,1,2:T(8,128)S(1)} %copy.220), kind=kOutput, calls=%fused_computation.4.clone.1 | convolution fusion | flops 33800192 | bytes 594432 | tf_op jit(solution)/shard_map/while/body/eval_jaxpr/tgbj,bjd->tgbd/dot_general | solution.py:31
  77.4 0.7 copy.121
  78.1 3.4 %all-to-all-start = ((f32[16,1,64]{2,1,0:T(1,128)}), f32[16,1,64]{2,1,0:T(1,128)S(1)}, u32[]{:S(2)}, u32[]{:S(2)}) async-start(f32[16,1,64]{2,1,0:T(1,128)} %copy.121), calls=%async_computation | async-start | bytes 16384 | tf_op jit(solution)/shard_map/all_to_all | solution.py:137
  81.5 2.2 %copy.161 = bf16[128,8,8,128]{3,2,1,0:T(8,128)(2,1)S(1)} copy(bf16[128,8,8,128]{3,1,2,0:T(8,128)(2,1)} %bitcast.194) | data formatting | bytes 4194304
  85.6 0.7 copy.125
  86.4 1.4 %all-to-all-done = f32[16,1,64]{2,1,0:T(1,128)S(1)} async-done(((f32[16,1,64]{2,1,0:T(1,128)}), f32[16,1,64]{2,1,0:T(1,128)S(1)}, u32[]{:S(2)}, u32[]{:S(2)}) %all-to-all-start) | async-done | bytes 4128 | tf_op jit(solution)/shard_map/all_to_all | solution.py:137
  87.9 4.6 %all-to-all-start.1 = ((f32[16,1,64]{2,1,0:T(1,128)}), f32[16,1,64]{2,1,0:T(1,128)S(1)}, u32[]{:S(2)}, u32[]{:S(2)}) async-start(f32[16,1,64]{2,1,0:T(1,128)} %copy.125), calls=%async_computation.1 | async-start | bytes 16384 | tf_op jit(solution)/shard_map/all_to_all | solution.py:138
  93.7 2.3 %reduce.15 = bf16[16,8192]{1,0:T(8,128)(2,1)S(1)} reduce(bf16[16,1,8192]{2,1,0:T(2,128)(2,1)S(1)} %reshape.281, bf16[]{:T(256)} %broadcast.113), dimensions={1}, to_apply=%reshape.281.reduce_sub_computation | reduce | bytes 524290 | tf_op jit(solution)/shard_map/reshape | solution.py:141
  96.0 0.9 reshape.294
  96.9 1.9 %all-to-all-done.1 = f32[16,1,64]{2,1,0:T(1,128)S(1)} async-done(((f32[16,1,64]{2,1,0:T(1,128)}), f32[16,1,64]{2,1,0:T(1,128)S(1)}, u32[]{:S(2)}, u32[]{:S(2)}) %all-to-all-start.1) | async-done | bytes 4128 | tf_op jit(solution)/shard_map/all_to_all | solution.py:138
  98.8 4.1 %all-to-all-start.2 = ((bf16[16,2,4096]{2,1,0:T(2,128)(2,1)}), bf16[16,2,4096]{2,1,0:T(2,128)(2,1)S(1)}, u32[]{:S(2)}, u32[]{:S(2)}) async-start(bf16[16,2,4096]{2,1,0:T(2,128)(2,1)} %reshape.294), calls=%async_computation.2 | async-start | bytes 524288 | tf_op jit(solution)/shard_map/all_to_all | solution.py:140
  103.0 10.0 %all-to-all-done.2 = bf16[16,2,4096]{2,1,0:T(2,128)(2,1)S(1)} async-done(((bf16[16,2,4096]{2,1,0:T(2,128)(2,1)}), bf16[16,2,4096]{2,1,0:T(2,128)(2,1)S(1)}, u32[]{:S(2)}, u32[]{:S(2)}) %all-to-all-start.2) | async-done | bytes 262176 | tf_op jit(solution)/shard_map/all_to_all | solution.py:140
  113.4 0.8 multiply_reduce_fusion.1
  114.3 0.7 divide_convert_fusion
  (149 shorter events, 18.6 us)
Async XLA Ops:
  0.0 29.1 %copy-start = (bf16[1,1024]{1,0:T(2,128)(2,1)S(1)}, bf16[1,1024]{1,0:T(2,128)(2,1)}, u32[]{:S(2)}) copy-start(bf16[1,1024]{1,0:T(2,128)(2,1)} %param.12) | copy-start | bytes 6148
  24.8 6.3 %copy-start.8 = (pred[2]{0:T(512)(128)(4,1)}, pred[2]{0:T(512)(128)(4,1)S(1)}, u32[]{:S(2)}) copy-start(pred[2]{0:T(512)(128)(4,1)S(1)} %get-tuple-element.152) | copy-start | bytes 10
  27.0 0.7 copy-start.11
  29.3 2.7 %copy-start.10 = (s32[1,32]{1,0:T(1,128)S(1)}, s32[1,32]{1,0:T(1,128)}, u32[]{:S(2)}) copy-start(s32[1,32]{1,0:T(1,128)} %param.18) | copy-start | bytes 388
  30.1 21.3 %copy-start.1 = (bf16[1024,1024]{1,0:T(8,128)(2,1)S(1)}, bf16[1024,1024]{1,0:T(8,128)(2,1)}, u32[]{:S(2)}) copy-start(bf16[1024,1024]{1,0:T(8,128)(2,1)} %param.14) | copy-start | bytes 6291460
  52.1 1.6 %copy-start.2 = (bf16[1024,1024]{1,0:T(8,128)(2,1)S(1)}, bf16[1024,1024]{1,0:T(8,128)(2,1)}, u32[]{:S(2)}) copy-start(bf16[1024,1024]{1,0:T(8,128)(2,1)} %param.15) | copy-start | bytes 6291460
  54.5 1.9 %copy-start.4 = (f32[8,16,8]{1,2,0:T(8,128)S(1)}, f32[8,16,8]{1,2,0:T(8,128)}, u32[]{:S(2)}) copy-start(f32[8,16,8]{1,2,0:T(8,128)} %custom-call) | copy-start | bytes 12292
  54.5 1.9 %copy-start.5 = (f32[8,16,8]{1,2,0:T(8,128)S(1)}, f32[8,16,8]{1,2,0:T(8,128)}, u32[]{:S(2)}) copy-start(f32[8,16,8]{1,2,0:T(8,128)} %custom-call.1) | copy-start | bytes 12292
  78.1 9.8 %all-to-all-start = ((f32[16,1,64]{2,1,0:T(1,128)}), f32[16,1,64]{2,1,0:T(1,128)S(1)}, u32[]{:S(2)}, u32[]{:S(2)}) async-start(f32[16,1,64]{2,1,0:T(1,128)} %copy.121), calls=%async_computation | async-start | bytes 16384 | tf_op jit(solution)/shard_map/all_to_all | solution.py:137
  83.8 0.7 copy-start.6
  83.8 0.9 copy-start.7
  83.8 1.0 copy-start.3
  84.7 0.7 copy-start.9
  87.9 10.9 %all-to-all-start.1 = ((f32[16,1,64]{2,1,0:T(1,128)}), f32[16,1,64]{2,1,0:T(1,128)S(1)}, u32[]{:S(2)}, u32[]{:S(2)}) async-start(f32[16,1,64]{2,1,0:T(1,128)} %copy.125), calls=%async_computation.1 | async-start | bytes 16384 | tf_op jit(solution)/shard_map/all_to_all | solution.py:138
  98.8 14.1 %all-to-all-start.2 = ((bf16[16,2,4096]{2,1,0:T(2,128)(2,1)}), bf16[16,2,4096]{2,1,0:T(2,128)(2,1)S(1)}, u32[]{:S(2)}, u32[]{:S(2)}) async-start(bf16[16,2,4096]{2,1,0:T(2,128)(2,1)} %reshape.294), calls=%async_computation.2 | async-start | bytes 524288 | tf_op jit(solution)/shard_map/all_to_all | solution.py:140
where the time goes:
time: 116 us; the launch traced here: 115 us
  blocking collectives  42.1 us (36%)
  local copies, waits for them, and re-layouts  18.6 us (16%)
  matrix products  14.9 us (13%)
  waiting for transfers between devices  13.3 us (11%)
  other arithmetic  13.2 us (11%)
  starting transfers between devices  12.1 us (10%)
    all_gather x1, blocking collectives, per_device(): gathered = lax.all_gather(queries, 'seq', axis=0, tiled=True)  24.8 us
    all_gather x1, blocking collectives, per_device(): every_list = lax.all_gather(keep_lists, 'seq', axis=0, tiled=True)  17.3 us
    unnamed x33, local copies, waits for them, and re-layouts  11.3 us
    dot_general x9, matrix products, block_terms(): jnp.einsum(form, weights.astype(jnp.bfloat16), value_rows, preferred_elem...  10.7 us
    all_to_all x1, waiting for transfers between devices, per_device(): lax.all_to_all(units.reshape(devices, 1, HEADS * HD), 'seq', split_axis=0...  9.97 us
    reduce_sum x9, other arithmetic, block_terms(): block_sum = jnp.sum(weights, axis=-1)  5.2 us
    all_to_all x1, starting transfers between devices, per_device(): lax.all_to_all(span_sum[:, None, :], 'seq', split_axis=0, concat_axis=1,...  4.59 us
    all_to_all x1, starting transfers between devices, per_device(): lax.all_to_all(units.reshape(devices, 1, HEADS * HD), 'seq', split_axis=0...  4.08 us
  transfers between devices with their start and end apart: 3, of which 3 were waited for; matrix products, arithmetic and copies ran while one was open for 8% of the time, Pallas kernels for 0%

commit v1 on v0

v1 whole, which is shorter than its diff:
```python
import functools
import math

import jax
import jax.numpy as jnp
from jax import lax
from jax.experimental import pallas as pl
from jax.experimental.pallas import tpu as pltpu
from jax.sharding import PartitionSpec as P

HD = 128
BLOCK = 128
LANES = 128
TOKENS = 16

DEAD = -1e30
FLOOR = -1e29
MESH = pl.DeviceIdType.MESH
COEF = HD ** (-0.5) * math.log2(math.e)
NT = (((1,), (1,)), ((), ()))
NN = (((1,), (0,)), ((), ()))


def softmax_terms(scores, bias, values):
    rows, group, keys = scores.shape
    masked = scores + bias
    top = jnp.maximum(jnp.max(masked, axis=-1, keepdims=True), FLOOR)
    weights = jnp.exp2((masked - top) * COEF)
    total = jnp.sum(weights, axis=-1, keepdims=True)
    out = lax.dot_general(
        weights.reshape(rows * group, keys).astype(jnp.bfloat16),
        values,
        NN,
        preferred_element_type=jnp.float32,
    )
    return top, total, out.reshape(rows, group, HD)


def kernel(
    n, kvh, group,
    len_ref, q_ref, nk_ref, nv_ref, keep_ref, dk_hbm, dv_hbm, sk_hbm, sv_hbm,
    out_ref,
    dk, dv, sk, sv, q_rows, q_all, lists, bias_ref, units, stats, suf_units, suf_stats,
    in_units, in_stats,
    load_sem, q_send, q_recv, l_send, l_recv, u_send, u_recv, s_send, s_recv, p_send, p_recv,
):
    part = lax.axis_index("parts")
    me = lax.axis_index("seq")
    row = me // 2
    parity = me % 2
    partner = me + 1 - 2 * parity
    heads = kvh * group
    keys = dk.shape[0]
    blocks = keys // BLOCK

    def peer_of(i):
        return lax.rem(2 * row + i + 1, n)

    loads = []
    for index, (source, target) in enumerate(((sk_hbm, sk), (sv_hbm, sv), (dk_hbm, dk), (dv_hbm, dv))):
        load = pltpu.make_async_copy(source, target, load_sem.at[index])
        load.start()
        loads.append(load)

    barrier = pltpu.get_barrier_semaphore()
    pl.semaphore_signal(barrier, inc=1, device_id=(part, partner), device_id_type=MESH)

    def greet(i, carry):
        pl.semaphore_signal(barrier, inc=1, device_id=(part, peer_of(i)), device_id_type=MESH)
        return carry

    lax.fori_loop(1, n - 1, greet, 0)

    for h in range(heads):
        q_rows[h : h + 1, :] = q_ref[0:1, h * HD : (h + 1) * HD].astype(jnp.float32)
    q_all[me] = q_rows[...].astype(jnp.bfloat16)
    kept = keep_ref.shape[1]
    width = lists.shape[2]
    ids = keep_ref[...]
    blank = jnp.full((1, kept), -1, jnp.int32)
    pieces = [jnp.where(parity == 0, ids, blank), jnp.where(parity == 1, ids, blank)]
    if width > 2 * kept:
        pieces.append(jnp.full((1, width - 2 * kept), -1, jnp.int32))
    lists[me] = jnp.broadcast_to(jnp.concatenate(pieces, axis=1), (8, width))

    pl.semaphore_wait(barrier, n - 1)

    def q_copy(peer, slot):
        return pltpu.make_async_remote_copy(
            src_ref=q_all.at[slot], dst_ref=q_all.at[slot],
            send_sem=q_send.at[peer], recv_sem=q_recv.at[slot],
            device_id=(part, peer), device_id_type=MESH,
        )

    def l_copy(peer, slot):
        return pltpu.make_async_remote_copy(
            src_ref=lists.at[slot], dst_ref=lists.at[slot],
            send_sem=l_send.at[peer], recv_sem=l_recv.at[slot],
            device_id=(part, peer), device_id_type=MESH,
        )

    def u_copy(peer, slot, target):
        return pltpu.make_async_remote_copy(
            src_ref=units.at[slot], dst_ref=in_units.at[target],
            send_sem=u_send.at[peer], recv_sem=u_recv.at[target],
            device_id=(part, peer), device_id_type=MESH,
        )

    def s_copy(peer, slot, target):
        return pltpu.make_async_remote_copy(
            src_ref=stats.at[slot], dst_ref=in_stats.at[target],
            send_sem=s_send.at[peer], recv_sem=s_recv.at[target],
            device_id=(part, peer), device_id_type=MESH,
        )

    q_copy(partner, me).start()
    l_copy(partner, me).start()

    def share(i, carry):
        q_copy(peer_of(i), me).start()
        l_copy(peer_of(i), me).start()
        return carry

    lax.fori_loop(1, n - 1, share, 0)

    lane = lax.broadcasted_iota(jnp.int32, (1, group, LANES), 2)
    position = parity * keys + lax.broadcasted_iota(jnp.int32, (1, group, keys), 2)
    suf_bias = jnp.where(position < len_ref[row], 0.0, DEAD)
    token = lax.broadcasted_iota(jnp.int32, (2, group, 1), 0)
    visible = token >= parity
    q_copy(partner, partner).wait_recv()
    loads[0].wait()
    loads[1].wait()
    stat = jnp.zeros((2, group, LANES), jnp.float32)
    for pair in range(kvh // 2):
        q_pair = q_all[pl.ds(2 * row, 2), 2 * group * pair : 2 * group * (pair + 1), :].astype(jnp.float32)
        made = []
        for half in range(2):
            h = 2 * pair + half
            cols = slice(h * HD, (h + 1) * HD)
            q_head = q_pair[:, half * group : (half + 1) * group, :]
            scores = lax.dot_general(
                q_head.reshape(2 * group, HD).astype(jnp.bfloat16), sk[:, cols], NT,
                preferred_element_type=jnp.float32,
            ).reshape(2, group, keys)
            top, total, out = softmax_terms(scores, suf_bias, sv[:, cols])
            new_key = nk_ref[0:1, cols].astype(jnp.float32).reshape(1, 1, HD)
            new_value = nv_ref[0:1, cols].astype(jnp.float32).reshape(1, 1, HD)
            own = jnp.where(visible, jnp.sum(q_head * new_key, axis=-1, keepdims=True), DEAD)
            joint = jnp.maximum(top, own)
            old_scale = jnp.exp2((top - joint) * COEF)
            own_scale = jnp.exp2((own - joint) * COEF)
            total = old_scale * total + own_scale
            out = old_scale * out + own_scale * new_value
            made.append(out / jnp.maximum(total, 1.0))
            stat = jnp.where(lane == h, joint, stat)
            stat = jnp.where(lane == kvh + h, total, stat)
        suf_units[:, 2 * group * pair : 2 * group * (pair + 1), :] = jnp.concatenate(made, axis=1).astype(jnp.bfloat16)
    suf_stats[...] = stat
    in_units[n] = suf_units[parity]
    in_stats[n] = suf_stats[parity]
    suffix_copies = [
        pltpu.make_async_remote_copy(
            src_ref=source.at[1 - parity], dst_ref=target.at[n + 1],
            send_sem=p_send.at[index], recv_sem=p_recv.at[index],
            device_id=(part, partner), device_id_type=MESH,
        )
        for index, (source, target) in enumerate(((suf_units, in_units), (suf_stats, in_stats)))
    ]
    for copy in suffix_copies:
        copy.start()

    l_copy(partner, partner).wait_recv()

    def arrive(i, carry):
        q_copy(peer_of(i), peer_of(i)).wait_recv()
        l_copy(peer_of(i), peer_of(i)).wait_recv()
        return carry

    lax.fori_loop(1, n - 1, arrive, 0)
    loads[2].wait()
    loads[3].wait()
    chunk = min(n, TOKENS)

    def span(start):
        both = lists[pl.ds(start, chunk)].reshape(chunk // 2, 2, 8, width)
        both = jnp.maximum(both[:, 0], both[:, 1])
        for b in range(blocks):
            hit = jnp.max(jnp.where(both == me * blocks + b, 0.0, DEAD), axis=-1, keepdims=True)
            bias_ref[:, :, b * BLOCK : (b + 1) * BLOCK] = jnp.broadcast_to(hit, (chunk // 2, 8, BLOCK))
        stat = jnp.zeros((chunk, group, LANES), jnp.float32)
        for pair in range(kvh // 2):
            q_pair = q_all[pl.ds(start, chunk), 2 * group * pair : 2 * group * (pair + 1), :].astype(jnp.float32)
            made = []
            for half in range(2):
                h = 2 * pair + half
                cols = slice(h * HD, (h + 1) * HD)
                q_head = q_pair[:, half * group : (half + 1) * group, :]
                scores = lax.dot_general(
                    q_head.reshape(chunk * group, HD).astype(jnp.bfloat16), dk[:, cols], NT,
                    preferred_element_type=jnp.float32,
                ).reshape(chunk, group, keys)
                bias = jnp.broadcast_to(
                    bias_ref[...][:, None], (chunk // 2, 2, group, keys)
                ).reshape(chunk, group, keys)
                top, total, out = softmax_terms(scores, bias, dv[:, cols])
                made.append(out * (1.0 / jnp.maximum(total, 1.0)))
                stat = jnp.where(lane == h, top, stat)
                stat = jnp.where(lane == kvh + h, total, stat)
            units[pl.ds(start, chunk), 2 * group * pair : 2 * group * (pair + 1), :] = jnp.concatenate(made, axis=1).astype(jnp.bfloat16)
        stats[pl.ds(start, chunk)] = stat

    if n > chunk:
        def step(c, carry):
            span(c * chunk)
            return carry

        lax.fori_loop(0, n // chunk, step, 0)
    else:
        span(0)

    def deliver(i, carry):
        s_copy(peer_of(i), peer_of(i), me).start()
        u_copy(peer_of(i), peer_of(i), me).start()
        return carry

    lax.fori_loop(1, n - 1, deliver, 0)
    s_copy(partner, partner, me).start()
    u_copy(partner, partner, me).start()
    in_units[me] = units[me]
    in_stats[me] = stats[me]
    q_copy(partner, me).wait_send()
    l_copy(partner, me).wait_send()

    def q_sent(i, carry):
        q_copy(peer_of(i), me).wait_send()
        l_copy(peer_of(i), me).wait_send()
        return carry

    lax.fori_loop(1, n - 1, q_sent, 0)
    for copy in suffix_copies:
        copy.wait()
    s_copy(partner, partner, partner).wait_recv()
    u_copy(partner, partner, partner).wait_recv()

    def collect(i, carry):
        s_copy(peer_of(i), peer_of(i), peer_of(i)).wait_recv()
        u_copy(peer_of(i), peer_of(i), peer_of(i)).wait_recv()
        return carry

    lax.fori_loop(1, n - 1, collect, 0)

    tops = in_stats[...]
    ceiling = jnp.max(tops, axis=0, keepdims=True)
    spread = jnp.exp2((tops - ceiling) * COEF)
    sums = pltpu.roll(tops.reshape((n + 2) * group, LANES), LANES - kvh, 1).reshape(n + 2, group, LANES)
    weight = spread * sums
    weight = weight / jnp.sum(weight, axis=0, keepdims=True)
    for pair in range(kvh // 2):
        parts = in_units[:, 2 * group * pair : 2 * group * (pair + 1), :].astype(jnp.float32)
        ends = []
        for half in range(2):
            h = 2 * pair + half
            ends.append(jnp.sum(weight[:, :, h : h + 1] * parts[:, half * group : (half + 1) * group, :], axis=0))
        out_ref[2 * group * pair : 2 * group * (pair + 1), :] = jnp.concatenate(ends, axis=0).astype(out_ref.dtype)

    s_copy(partner, partner, me).wait_send()
    u_copy(partner, partner, me).wait_send()

    def u_sent(i, carry):
        s_copy(peer_of(i), peer_of(i), me).wait_send()
        u_copy(peer_of(i), peer_of(i), me).wait_send()
        return carry

    lax.fori_loop(1, n - 1, u_sent, 0)


def per_device(n, queries, new_keys, new_values, doc_keys, doc_values, suffix_keys, suffix_values, keep_lists, suffix_lengths):
    heads = queries.shape[1] // HD
    kvh = new_keys.shape[1] // HD
    group = heads // kvh
    width = -(-2 * keep_lists.shape[1] // LANES) * LANES
    keys, columns = doc_keys.shape
    vmem = pl.BlockSpec(memory_space=pltpu.VMEM)
    smem = pl.BlockSpec(memory_space=pltpu.SMEM)
    anywhere = pl.BlockSpec(memory_space=pl.ANY)
    dma = pltpu.SemaphoreType.DMA
    out = pl.pallas_call(
        functools.partial(kernel, n, kvh, group),
        out_shape=jax.ShapeDtypeStruct((heads, HD), jnp.bfloat16),
        in_specs=[smem, vmem, vmem, vmem, vmem, anywhere, anywhere, anywhere, anywhere],
        out_specs=vmem,
        scratch_shapes=[
            pltpu.VMEM((keys, columns), jnp.bfloat16),
            pltpu.VMEM((keys, columns), jnp.bfloat16),
            pltpu.VMEM(suffix_keys.shape, jnp.bfloat16),
            pltpu.VMEM(suffix_keys.shape, jnp.bfloat16),
            pltpu.VMEM((heads, HD), jnp.float32),
            pltpu.VMEM((n, heads, HD), jnp.bfloat16),
            pltpu.VMEM((n, 8, width), jnp.int32),
            pltpu.VMEM((min(n, TOKENS) // 2, 8, keys), jnp.float32),
            pltpu.VMEM((n, heads, HD), jnp.bfloat16),
            pltpu.VMEM((n, group, LANES), jnp.float32),
            pltpu.VMEM((2, heads, HD), jnp.bfloat16),
            pltpu.VMEM((2, group, LANES), jnp.float32),
            pltpu.VMEM((n + 2, heads, HD), jnp.bfloat16),
            pltpu.VMEM((n + 2, group, LANES), jnp.float32),
            dma((4,)),
            dma((n,)), dma((n,)), dma((n,)), dma((n,)),
            dma((n,)), dma((n,)), dma((n,)), dma((n,)),
            dma((2,)), dma((2,)),
        ],
        compiler_params=pltpu.CompilerParams(
            collective_id=0, has_side_effects=True, vmem_limit_bytes=48 * 1024 * 1024
        ),
    )(suffix_lengths, queries, new_keys, new_values, keep_lists, doc_keys, doc_values, suffix_keys, suffix_values)
    return out.reshape(1, heads * HD)


def solution(mesh):
    rows = P(("parts", "seq"), None)
    return jax.shard_map(
        functools.partial(per_device, mesh.shape["seq"]),
        mesh=mesh,
        in_specs=(rows,) * 8 + (P("parts"),),
        out_specs=rows,
        check_vma=False,
    )
```

time: 116 us -> 34.1 us (0.29)
  the two profiles are of different devices: /device:TPU:0 before, /device:TPU:25 now
where the time goes in v1:
time: 34.1 us; the launch traced here: 33.8 us
  Pallas kernels  26.5 us (78%)
  local copies, waits for them, and re-layouts  7.26 us (21%)
    pallas_call x1, Pallas kernels, per_device(): pl.pallas_call(functools.partial(kernel, n, kvh, group), out_shape=jax.Sh...  26.5 us
    unnamed x15, local copies, waits for them, and re-layouts  7.26 us

profile of v1, /device:TPU:25, one launch (start us, length us, event | category | flops | bytes accessed | tf_op | source)
XLA Modules:
  0.0 33.8 jit_solution(5377422825198262405)
XLA Ops:
  0.0 0.0 copy-start
  0.0 1.6 %copy-done = bf16[1024,1024]{1,0:T(8,128)(2,1)S(1)} copy-done((bf16[1024,1024]{1,0:T(8,128)(2,1)S(1)}, bf16[1024,1024]{1,0:T(8,128)(2,1)}, u32[]{:S(2)}) %copy-start) | copy-done | bytes 2097176
  1.6 0.0 copy-start.1
  1.6 1.6 %copy-done.1 = bf16[1024,1024]{1,0:T(8,128)(2,1)S(1)} copy-done((bf16[1024,1024]{1,0:T(8,128)(2,1)S(1)}, bf16[1024,1024]{1,0:T(8,128)(2,1)}, u32[]{:S(2)}) %copy-start.1) | copy-done | bytes 2097176
  3.2 0.0 copy-start.2
  3.2 0.8 %copy-done.2 = bf16[1,8192]{1,0:T(2,128)(2,1)S(1)} copy-done((bf16[1,8192]{1,0:T(2,128)(2,1)S(1)}, bf16[1,8192]{1,0:T(2,128)(2,1)}, u32[]{:S(2)}) %copy-start.2) | copy-done | bytes 16408
  3.9 0.0 copy-start.3
  3.9 0.7 %copy-done.3 = bf16[1,1024]{1,0:T(2,128)(2,1)S(1)} copy-done((bf16[1,1024]{1,0:T(2,128)(2,1)S(1)}, bf16[1,1024]{1,0:T(2,128)(2,1)}, u32[]{:S(2)}) %copy-start.3) | copy-done | bytes 2072
  4.6 0.0 copy-start.4
  4.6 0.7 %copy-done.4 = bf16[1,1024]{1,0:T(2,128)(2,1)S(1)} copy-done((bf16[1,1024]{1,0:T(2,128)(2,1)S(1)}, bf16[1,1024]{1,0:T(2,128)(2,1)}, u32[]{:S(2)}) %copy-start.4) | copy-done | bytes 2072
  5.3 0.0 copy-start.5
  5.3 0.7 %copy-done.5 = s32[8]{0:T(128)S(1)} copy-done((s32[8]{0:T(128)S(1)}, s32[8]{0:T(128)}, u32[]{:S(2)}) %copy-start.5) | copy-done | bytes 56
  6.0 0.0 copy-start.6
  6.0 0.7 %copy-done.6 = s32[1,32]{1,0:T(1,128)S(1)} copy-done((s32[1,32]{1,0:T(1,128)S(1)}, s32[1,32]{1,0:T(1,128)}, u32[]{:S(2)}) %copy-start.6) | copy-done | bytes 152
  6.6 26.5 %shard_map.91 = bf16[64,128]{1,0:T(8,128)(2,1)S(1)} custom-call(s32[8]{0:T(128)S(1)} %copy-done.5, bf16[1,8192]{1,0:T(2,128)(2,1)S(1)} %copy-done.2, bf16[1,1024]{1,0:T(2,128)(2,1)S(1)} %copy-done.3, bf16[1,1024]{1,0:T(2,128)(2,1)S(1)} %copy-done.4, s32[1,32]{1,0:T(1,128)S(1)} %copy-done.6, bf16[1024,1024]{1,0:T(8,128)(2,1)S(1)} %copy-done, ...), custom_call_target="tpu_custom_call" | custom-call | tf_op jit(solution)/shard_map/pallas_call | solution.py:288
  33.2 0.6 %copy.12 = bf16[1,1,64,128]{3,1,2,0:T(2,128)(2,1)} copy(bf16[1,1,64,128]{3,2,1,0:T(8,128)(2,1)S(1)} %bitcast.5) | data formatting | bytes 32768
Async XLA Ops:
  0.0 1.6 %copy-start = (bf16[1024,1024]{1,0:T(8,128)(2,1)S(1)}, bf16[1024,1024]{1,0:T(8,128)(2,1)}, u32[]{:S(2)}) copy-start(bf16[1024,1024]{1,0:T(8,128)(2,1)} %dk_hbm.1) | copy-start | bytes 6291460
  1.6 1.6 %copy-start.1 = (bf16[1024,1024]{1,0:T(8,128)(2,1)S(1)}, bf16[1024,1024]{1,0:T(8,128)(2,1)}, u32[]{:S(2)}) copy-start(bf16[1024,1024]{1,0:T(8,128)(2,1)} %dv_hbm.1) | copy-start | bytes 6291460
  3.2 0.8 %copy-start.2 = (bf16[1,8192]{1,0:T(2,128)(2,1)S(1)}, bf16[1,8192]{1,0:T(2,128)(2,1)}, u32[]{:S(2)}) copy-start(bf16[1,8192]{1,0:T(2,128)(2,1)} %q_ref.1) | copy-start | bytes 49156
  3.9 0.7 %copy-start.3 = (bf16[1,1024]{1,0:T(2,128)(2,1)S(1)}, bf16[1,1024]{1,0:T(2,128)(2,1)}, u32[]{:S(2)}) copy-start(bf16[1,1024]{1,0:T(2,128)(2,1)} %nk_ref.1) | copy-start | bytes 6148
  4.6 0.7 %copy-start.4 = (bf16[1,1024]{1,0:T(2,128)(2,1)S(1)}, bf16[1,1024]{1,0:T(2,128)(2,1)}, u32[]{:S(2)}) copy-start(bf16[1,1024]{1,0:T(2,128)(2,1)} %nv_ref.1) | copy-start | bytes 6148
  5.3 0.7 %copy-start.5 = (s32[8]{0:T(128)S(1)}, s32[8]{0:T(128)}, u32[]{:S(2)}) copy-start(s32[8]{0:T(128)} %len_ref.1) | copy-start | bytes 100
  6.0 0.7 %copy-start.6 = (s32[1,32]{1,0:T(1,128)S(1)}, s32[1,32]{1,0:T(1,128)}, u32[]{:S(2)}) copy-start(s32[1,32]{1,0:T(1,128)} %keep_ref.1) | copy-start | bytes 388

commit v2 on v1

--- a/solution.py
+++ b/solution.py
@@ -38,8 +38,9 @@
 
 def kernel(
     n, kvh, group,
-    len_ref, q_ref, nk_ref, nv_ref, keep_ref, dk_hbm, dv_hbm, sk_hbm, sv_hbm,
+    len_hbm, q_hbm, nk_hbm, nv_hbm, keep_hbm, dk_hbm, dv_hbm, sk_hbm, sv_hbm,
     out_ref,
+    len_ref, q_ref, nk_ref, nv_ref, keep_ref,
     dk, dv, sk, sv, q_rows, q_all, lists, bias_ref, units, stats, suf_units, suf_stats,
     in_units, in_stats,
     load_sem, q_send, q_recv, l_send, l_recv, u_send, u_recv, s_send, s_recv, p_send, p_recv,
@@ -57,7 +58,11 @@
         return lax.rem(2 * row + i + 1, n)
 
     loads = []
-    for index, (source, target) in enumerate(((sk_hbm, sk), (sv_hbm, sv), (dk_hbm, dk), (dv_hbm, dv))):
+    pairs = (
+        (q_hbm, q_ref), (keep_hbm, keep_ref), (len_hbm, len_ref), (nk_hbm, nk_ref), (nv_hbm, nv_ref),
+        (sk_hbm, sk), (sv_hbm, sv), (dk_hbm, dk), (dv_hbm, dv),
+    )
+    for index, (source, target) in enumerate(pairs):
         load = pltpu.make_async_copy(source, target, load_sem.at[index])
         load.start()
         loads.append(load)
@@ -71,11 +76,13 @@
 
     lax.fori_loop(1, n - 1, greet, 0)
 
+    loads[0].wait()
     for h in range(heads):
         q_rows[h : h + 1, :] = q_ref[0:1, h * HD : (h + 1) * HD].astype(jnp.float32)
     q_all[me] = q_rows[...].astype(jnp.bfloat16)
     kept = keep_ref.shape[1]
     width = lists.shape[2]
+    loads[1].wait()
     ids = keep_ref[...]
     blank = jnp.full((1, kept), -1, jnp.int32)
     pieces = [jnp.where(parity == 0, ids, blank), jnp.where(parity == 1, ids, blank)]
@@ -123,14 +130,17 @@
 
     lax.fori_loop(1, n - 1, share, 0)
 
+    loads[2].wait()
+    loads[3].wait()
+    loads[4].wait()
     lane = lax.broadcasted_iota(jnp.int32, (1, group, LANES), 2)
     position = parity * keys + lax.broadcasted_iota(jnp.int32, (1, group, keys), 2)
     suf_bias = jnp.where(position < len_ref[row], 0.0, DEAD)
     token = lax.broadcasted_iota(jnp.int32, (2, group, 1), 0)
     visible = token >= parity
     q_copy(partner, partner).wait_recv()
-    loads[0].wait()
-    loads[1].wait()
+    loads[5].wait()
+    loads[6].wait()
     stat = jnp.zeros((2, group, LANES), jnp.float32)
     for pair in range(kvh // 2):
         q_pair = q_all[pl.ds(2 * row, 2), 2 * group * pair : 2 * group * (pair + 1), :].astype(jnp.float32)
@@ -178,8 +188,8 @@
         return carry
 
     lax.fori_loop(1, n - 1, arrive, 0)
-    loads[2].wait()
-    loads[3].wait()
+    loads[7].wait()
+    loads[8].wait()
     chunk = min(n, TOKENS)
 
     def span(start):
@@ -281,16 +291,19 @@
     group = heads // kvh
     width = -(-2 * keep_lists.shape[1] // LANES) * LANES
     keys, columns = doc_keys.shape
-    vmem = pl.BlockSpec(memory_space=pltpu.VMEM)
-    smem = pl.BlockSpec(memory_space=pltpu.SMEM)
-    anywhere = pl.BlockSpec(memory_space=pl.ANY)
+    hbm = pl.BlockSpec(memory_space=pltpu.HBM)
     dma = pltpu.SemaphoreType.DMA
     out = pl.pallas_call(
         functools.partial(kernel, n, kvh, group),
         out_shape=jax.ShapeDtypeStruct((heads, HD), jnp.bfloat16),
-        in_specs=[smem, vmem, vmem, vmem, vmem, anywhere, anywhere, anywhere, anywhere],
-        out_specs=vmem,
+        in_specs=[hbm] * 9,
+        out_specs=pl.BlockSpec(memory_space=pltpu.VMEM),
         scratch_shapes=[
+            pltpu.SMEM(suffix_lengths.shape, jnp.int32),
+            pltpu.VMEM(queries.shape, jnp.bfloat16),
+            pltpu.VMEM(new_keys.shape, jnp.bfloat16),
+            pltpu.VMEM(new_values.shape, jnp.bfloat16),
+            pltpu.VMEM(keep_lists.shape, jnp.int32),
             pltpu.VMEM((keys, columns), jnp.bfloat16),
             pltpu.VMEM((keys, columns), jnp.bfloat16),
             pltpu.VMEM(suffix_keys.shape, jnp.bfloat16),
@@ -305,13 +318,13 @@
             pltpu.VMEM((2, group, LANES), jnp.float32),
             pltpu.VMEM((n + 2, heads, HD), jnp.bfloat16),
             pltpu.VMEM((n + 2, group, LANES), jnp.float32),
-            dma((4,)),
+            dma((9,)),
             dma((n,)), dma((n,)), dma((n,)), dma((n,)),
             dma((n,)), dma((n,)), dma((n,)), dma((n,)),
             dma((2,)), dma((2,)),
         ],
         compiler_params=pltpu.CompilerParams(
-            collective_id=0, has_side_effects=True, vmem_limit_bytes=48 * 1024 * 1024
+            collective_id=0, has_side_effects=True, vmem_limit_bytes=65000 * 1024
         ),
     )(suffix_lengths, queries, new_keys, new_values, keep_lists, doc_keys, doc_values, suffix_keys, suffix_values)
     return out.reshape(1, heads * HD)

time: 34.1 us -> 27.9 us (0.82)
  local copies, waits for them, and re-layouts: 7.26 us -> 1.36 us
    unnamed x15 -> x1, local copies, waits for them, and re-layouts: 7.26 us -> 1.36 us
where the time goes in v2:
time: 27.9 us; the launch traced here: 27.6 us
  Pallas kernels  26.3 us (94%)
  local copies, waits for them, and re-layouts  1.36 us (5%)
    pallas_call x1, Pallas kernels, per_device(): pl.pallas_call(functools.partial(kernel, n, kvh, group), out_shape=jax.Sh...  26.3 us
    unnamed x1, local copies, waits for them, and re-layouts  1.36 us

profile of v2, /device:TPU:25, one launch (start us, length us, event | category | flops | bytes accessed | tf_op | source)
XLA Modules:
  0.0 27.6 jit_solution(17208941783463968706)
XLA Ops:
  0.0 26.3 %shard_map.91 = bf16[64,128]{1,0:T(8,128)(2,1)} custom-call(s32[8]{0:T(128)} %len_hbm.1, bf16[1,8192]{1,0:T(2,128)(2,1)} %q_hbm.1, bf16[1,1024]{1,0:T(2,128)(2,1)} %nk_hbm.1, bf16[1,1024]{1,0:T(2,128)(2,1)} %nv_hbm.1, s32[1,32]{1,0:T(1,128)} %keep_hbm.1, bf16[1024,1024]{1,0:T(8,128)(2,1)} %dk_hbm.1, bf16[1024,1024]{1,0:T(8,128)(2,1)} %dv_hbm.1, ...), custom_call_target="tpu_custom_call" | custom-call | tf_op jit(solution)/shard_map/pallas_call | solution.py:296
  26.3 1.4 %copy.12 = bf16[1,1,64,128]{3,1,2,0:T(2,128)(2,1)} copy(bf16[1,1,64,128]{3,2,1,0:T(8,128)(2,1)} %bitcast.5) | data formatting | bytes 32768

commit v3 on v2

--- a/solution.py
+++ b/solution.py
@@ -41,21 +41,22 @@
     len_hbm, q_hbm, nk_hbm, nv_hbm, keep_hbm, dk_hbm, dv_hbm, sk_hbm, sv_hbm,
     out_ref,
     len_ref, q_ref, nk_ref, nv_ref, keep_ref,
-    dk, dv, sk, sv, q_rows, q_all, lists, bias_ref, units, stats, suf_units, suf_stats,
+    dk, dv, sk, sv, q_rows, q_all, lists, bias_ref, units, stats, mate_units, mate_stats, merged, merged_stats, suf_units, suf_stats,
     in_units, in_stats,
-    load_sem, q_send, q_recv, l_send, l_recv, u_send, u_recv, s_send, s_recv, p_send, p_recv,
+    load_sem, q_send, q_recv, l_send, l_recv, m_send, m_recv, u_send, u_recv, s_send, s_recv, p_send, p_recv,
 ):
     part = lax.axis_index("parts")
     me = lax.axis_index("seq")
     row = me // 2
     parity = me % 2
     partner = me + 1 - 2 * parity
+    chips = n // 2
     heads = kvh * group
     keys = dk.shape[0]
     blocks = keys // BLOCK
 
     def peer_of(i):
-        return lax.rem(2 * row + i + 1, n)
+        return lax.rem(me + 2 * i, n)
 
     loads = []
     pairs = (
@@ -74,7 +75,7 @@
         pl.semaphore_signal(barrier, inc=1, device_id=(part, peer_of(i)), device_id_type=MESH)
         return carry
 
-    lax.fori_loop(1, n - 1, greet, 0)
+    lax.fori_loop(1, chips, greet, 0)
 
     loads[0].wait()
     for h in range(heads):
@@ -88,47 +89,62 @@
     pieces = [jnp.where(parity == 0, ids, blank), jnp.where(parity == 1, ids, blank)]
     if width > 2 * kept:
         pieces.append(jnp.full((1, width - 2 * kept), -1, jnp.int32))
-    lists[me] = jnp.broadcast_to(jnp.concatenate(pieces, axis=1), (8, width))
-
-    pl.semaphore_wait(barrier, n - 1)
-
-    def q_copy(peer, slot):
+    lists[me] = jnp.concatenate(pieces, axis=1)
+
+    pl.semaphore_wait(barrier, chips)
+
+    def q_copy(device, slot, send):
         return pltpu.make_async_remote_copy(
             src_ref=q_all.at[slot], dst_ref=q_all.at[slot],
-            send_sem=q_send.at[peer], recv_sem=q_recv.at[slot],
-            device_id=(part, peer), device_id_type=MESH,
-        )
-
-    def l_copy(peer, slot):
+            send_sem=q_send.at[send], recv_sem=q_recv.at[slot],
+            device_id=(part, device), device_id_type=MESH,
+        )
+
+    def l_copy(device, slot, send):
         return pltpu.make_async_remote_copy(
             src_ref=lists.at[slot], dst_ref=lists.at[slot],
-            send_sem=l_send.at[peer], recv_sem=l_recv.at[slot],
-            device_id=(part, peer), device_id_type=MESH,
-        )
-
-    def u_copy(peer, slot, target):
-        return pltpu.make_async_remote_copy(
-            src_ref=units.at[slot], dst_ref=in_units.at[target],
-            send_sem=u_send.at[peer], recv_sem=u_recv.at[target],
-            device_id=(part, peer), device_id_type=MESH,
-        )
-
-    def s_copy(peer, slot, target):
-        return pltpu.make_async_remote_copy(
-            src_ref=stats.at[slot], dst_ref=in_stats.at[target],
-            send_sem=s_send.at[peer], recv_sem=s_recv.at[target],
-            device_id=(part, peer), device_id_type=MESH,
-        )
-
-    q_copy(partner, me).start()
-    l_copy(partner, me).start()
+            send_sem=l_send.at[send], recv_sem=l_recv.at[slot],
+            device_id=(part, device), device_id_type=MESH,
+        )
+
+    def mate_copy(pair):
+        rows = slice(2 * group * pair, 2 * group * (pair + 1))
+        return pltpu.make_async_remote_copy(
+            src_ref=units.at[1 - parity, :, rows, :], dst_ref=mate_units.at[:, rows, :],
+            send_sem=m_send.at[pair], recv_sem=m_recv.at[pair],
+            device_id=(part, partner), device_id_type=MESH,
+        )
+
+    def mate_stats_copy():
+        return pltpu.make_async_remote_copy(
+            src_ref=stats.at[1 - parity], dst_ref=mate_stats,
+            send_sem=m_send.at[kvh // 2], recv_sem=m_recv.at[kvh // 2],
+            device_id=(part, partner), device_id_type=MESH,
+        )
+
+    def u_copy(device, target):
+        return pltpu.make_async_remote_copy(
+            src_ref=merged.at[device // 2], dst_ref=in_units.at[target],
+            send_sem=u_send.at[device // 2], recv_sem=u_recv.at[target],
+            device_id=(part, device), device_id_type=MESH,
+        )
+
+    def s_copy(device, target):
+        return pltpu.make_async_remote_copy(
+            src_ref=merged_stats.at[device // 2], dst_ref=in_stats.at[target],
+            send_sem=s_send.at[device // 2], recv_sem=s_recv.at[target],
+            device_id=(part, device), device_id_type=MESH,
+        )
+
+    q_copy(partner, me, partner).start()
+    l_copy(partner, me, partner).start()
 
     def share(i, carry):
-        q_copy(peer_of(i), me).start()
-        l_copy(peer_of(i), me).start()
-        return carry
-
-    lax.fori_loop(1, n - 1, share, 0)
+        q_copy(peer_of(i), me, peer_of(i)).start()
+        l_copy(peer_of(i), me, peer_of(i)).start()
+        return carry
+
+    lax.fori_loop(1, chips, share, 0)
 
     loads[2].wait()
     loads[3].wait()
@@ -138,7 +154,7 @@
     suf_bias = jnp.where(position < len_ref[row], 0.0, DEAD)
     token = lax.broadcasted_iota(jnp.int32, (2, group, 1), 0)
     visible = token >= parity
-    q_copy(partner, partner).wait_recv()
+    q_copy(partner, partner, me).wait_recv()
     loads[5].wait()
     loads[6].wait()
     stat = jnp.zeros((2, group, LANES), jnp.float32)
@@ -167,11 +183,11 @@
             stat = jnp.where(lane == kvh + h, total, stat)
         suf_units[:, 2 * group * pair : 2 * group * (pair + 1), :] = jnp.concatenate(made, axis=1).astype(jnp.bfloat16)
     suf_stats[...] = stat
-    in_units[n] = suf_units[parity]
-    in_stats[n] = suf_stats[parity]
+    in_units[chips] = suf_units[parity]
+    in_stats[chips] = suf_stats[parity]
     suffix_copies = [
         pltpu.make_async_remote_copy(
-            src_ref=source.at[1 - parity], dst_ref=target.at[n + 1],
+            src_ref=source.at[1 - parity], dst_ref=target.at[chips + 1],
             send_sem=p_send.at[index], recv_sem=p_recv.at[index],
             device_id=(part, partner), device_id_type=MESH,
         )
@@ -180,20 +196,31 @@
     for copy in suffix_copies:
         copy.start()
 
-    l_copy(partner, partner).wait_recv()
+    l_copy(partner, partner, me).wait_recv()
+    flip = 1 - 2 * parity
+
+    def forward(i, carry):
+        slot = peer_of(i)
+        q_copy(partner, slot, slot + flip).wait_recv()
+        q_copy(partner, slot, slot + flip).start()
+        l_copy(partner, slot, slot + flip).wait_recv()
+        l_copy(partner, slot, slot + flip).start()
+        return carry
+
+    lax.fori_loop(1, chips, forward, 0)
 
     def arrive(i, carry):
-        q_copy(peer_of(i), peer_of(i)).wait_recv()
-        l_copy(peer_of(i), peer_of(i)).wait_recv()
-        return carry
-
-    lax.fori_loop(1, n - 1, arrive, 0)
+        q_copy(partner, peer_of(i) + flip, me).wait_recv()
+        l_copy(partner, peer_of(i) + flip, me).wait_recv()
+        return carry
+
+    lax.fori_loop(1, chips, arrive, 0)
     loads[7].wait()
     loads[8].wait()
     chunk = min(n, TOKENS)
 
     def span(start):
-        both = lists[pl.ds(start, chunk)].reshape(chunk // 2, 2, 8, width)
+        both = lists[pl.ds(start, chunk)].reshape(chunk // 2, 2, 1, width)
         both = jnp.maximum(both[:, 0], both[:, 1])
         for b in range(blocks):
             hit = jnp.max(jnp.where(both == me * blocks + b, 0.0, DEAD), axis=-1, keepdims=True)
@@ -217,8 +244,14 @@
                 made.append(out * (1.0 / jnp.maximum(total, 1.0)))
                 stat = jnp.where(lane == h, top, stat)
                 stat = jnp.where(lane == kvh + h, total, stat)
-            units[pl.ds(start, chunk), 2 * group * pair : 2 * group * (pair + 1), :] = jnp.concatenate(made, axis=1).astype(jnp.bfloat16)
-        stats[pl.ds(start, chunk)] = stat
+            unit = jnp.concatenate(made, axis=1).astype(jnp.bfloat16).reshape(chunk // 2, 2, 2 * group, HD)
+            for side in range(2):
+                units[side, pl.ds(start // 2, chunk // 2), 2 * group * pair : 2 * group * (pair + 1), :] = unit[:, side]
+            if n == chunk:
+                mate_copy(pair).start()
+        stat = stat.reshape(chunk // 2, 2, group, LANES)
+        for side in range(2):
+            stats[side, pl.ds(start // 2, chunk // 2)] = stat[:, side]
 
     if n > chunk:
         def step(c, carry):
@@ -226,45 +259,76 @@
             return carry
 
         lax.fori_loop(0, n // chunk, step, 0)
+        for pair in range(kvh // 2):
+            mate_copy(pair).start()
     else:
         span(0)
 
+    mate_stats_copy().start()
+
+    mate_stats_copy().wait()
+    mine, other = stats[parity], mate_stats[...]
+
+    def aligned(values):
+        return pltpu.roll(values.reshape(-1, LANES), LANES - kvh, 1).reshape(values.shape)
+
+    joint = jnp.maximum(mine, other)
+    mine_part = jnp.exp2((mine - joint) * COEF) * aligned(mine)
+    other_part = jnp.exp2((other - joint) * COEF) * aligned(other)
+    total = mine_part + other_part
+    shares = 1.0 / jnp.maximum(total, 1.0)
+    mine_part = mine_part * shares
+    other_part = other_part * shares
+    shifted = pltpu.roll(total.reshape(-1, LANES), kvh, 1).reshape(total.shape)
+    merged_stats[...] = jnp.where(lane < kvh, joint, shifted)
+    for pair in range(kvh // 2):
+        rows = slice(2 * group * pair, 2 * group * (pair + 1))
+        mate_copy(pair).wait()
+        first = units[parity, :, rows, :].astype(jnp.float32)
+        second = mate_units[:, rows, :].astype(jnp.float32)
+        made = []
+        for half in range(2):
+            h = 2 * pair + half
+            part_rows = slice(half * group, (half + 1) * group)
+            made.append(
+                mine_part[:, :, h : h + 1] * first[:, part_rows, :]
+                + other_part[:, :, h : h + 1] * second[:, part_rows, :]
+            )
+        merged[:, rows, :] = jnp.concatenate(made, axis=1).astype(jnp.bfloat16)
+
     def deliver(i, carry):
-        s_copy(peer_of(i), peer_of(i), me).start()
-        u_copy(peer_of(i), peer_of(i), me).start()
-        return carry
-
-    lax.fori_loop(1, n - 1, deliver, 0)
-    s_copy(partner, partner, me).start()
-    u_copy(partner, partner, me).start()
-    in_units[me] = units[me]
-    in_stats[me] = stats[me]
-    q_copy(partner, me).wait_send()
-    l_copy(partner, me).wait_send()
+        s_copy(peer_of(i), row).start()
+        u_copy(peer_of(i), row).start()
+        return carry
+
+    lax.fori_loop(1, chips, deliver, 0)
+    in_units[row] = merged[row]
+    in_stats[row] = merged_stats[row]
+    q_copy(partner, me, partner).wait_send()
+    l_copy(partner, me, partner).wait_send()
 
     def q_sent(i, carry):
-        q_copy(peer_of(i), me).wait_send()
-        l_copy(peer_of(i), me).wait_send()
-        return carry
-
-    lax.fori_loop(1, n - 1, q_sent, 0)
+        q_copy(peer_of(i), me, peer_of(i)).wait_send()
+        l_copy(peer_of(i), me, peer_of(i)).wait_send()
+        q_copy(partner, peer_of(i), peer_of(i) + flip).wait_send()
+        l_copy(partner, peer_of(i), peer_of(i) + flip).wait_send()
+        return carry
+
+    lax.fori_loop(1, chips, q_sent, 0)
     for copy in suffix_copies:
         copy.wait()
-    s_copy(partner, partner, partner).wait_recv()
-    u_copy(partner, partner, partner).wait_recv()
 
     def collect(i, carry):
-        s_copy(peer_of(i), peer_of(i), peer_of(i)).wait_recv()
-        u_copy(peer_of(i), peer_of(i), peer_of(i)).wait_recv()
-        return carry
-
-    lax.fori_loop(1, n - 1, collect, 0)
+        s_copy(peer_of(i), peer_of(i) // 2).wait_recv()
+        u_copy(peer_of(i), peer_of(i) // 2).wait_recv()
+        return carry
+
+    lax.fori_loop(1, chips, collect, 0)
 
     tops = in_stats[...]
     ceiling = jnp.max(tops, axis=0, keepdims=True)
     spread = jnp.exp2((tops - ceiling) * COEF)
-    sums = pltpu.roll(tops.reshape((n + 2) * group, LANES), LANES - kvh, 1).reshape(n + 2, group, LANES)
-    weight = spread * sums
+    weight = spread * aligned(tops)
     weight = weight / jnp.sum(weight, axis=0, keepdims=True)
     for pair in range(kvh // 2):
         parts = in_units[:, 2 * group * pair : 2 * group * (pair + 1), :].astype(jnp.float32)
@@ -274,15 +338,12 @@
             ends.append(jnp.sum(weight[:, :, h : h + 1] * parts[:, half * group : (half + 1) * group, :], axis=0))
         out_ref[2 * group * pair : 2 * group * (pair + 1), :] = jnp.concatenate(ends, axis=0).astype(out_ref.dtype)
 
-    s_copy(partner, partner, me).wait_send()
-    u_copy(partner, partner, me).wait_send()
-
     def u_sent(i, carry):
-        s_copy(peer_of(i), peer_of(i), me).wait_send()
-        u_copy(peer_of(i), peer_of(i), me).wait_send()
-        return carry
-
-    lax.fori_loop(1, n - 1, u_sent, 0)
+        s_copy(peer_of(i), row).wait_send()
+        u_copy(peer_of(i), row).wait_send()
+        return carry
+
+    lax.fori_loop(1, chips, u_sent, 0)
 
 
 def per_device(n, queries, new_keys, new_values, doc_keys, doc_values, suffix_keys, suffix_values, keep_lists, suffix_lengths):
@@ -310,17 +371,22 @@
             pltpu.VMEM(suffix_keys.shape, jnp.bfloat16),
             pltpu.VMEM((heads, HD), jnp.float32),
             pltpu.VMEM((n, heads, HD), jnp.bfloat16),
-            pltpu.VMEM((n, 8, width), jnp.int32),
+            pltpu.VMEM((n, 1, width), jnp.int32),
             pltpu.VMEM((min(n, TOKENS) // 2, 8, keys), jnp.float32),
-            pltpu.VMEM((n, heads, HD), jnp.bfloat16),
-            pltpu.VMEM((n, group, LANES), jnp.float32),
+            pltpu.VMEM((2, n // 2, heads, HD), jnp.bfloat16),
+            pltpu.VMEM((2, n // 2, group, LANES), jnp.float32),
+            pltpu.VMEM((n // 2, heads, HD), jnp.bfloat16),
+            pltpu.VMEM((n // 2, group, LANES), jnp.float32),
+            pltpu.VMEM((n // 2, heads, HD), jnp.bfloat16),
+            pltpu.VMEM((n // 2, group, LANES), jnp.float32),
             pltpu.VMEM((2, heads, HD), jnp.bfloat16),
             pltpu.VMEM((2, group, LANES), jnp.float32),
-            pltpu.VMEM((n + 2, heads, HD), jnp.bfloat16),
-            pltpu.VMEM((n + 2, group, LANES), jnp.float32),
+            pltpu.VMEM((n // 2 + 2, heads, HD), jnp.bfloat16),
+            pltpu.VMEM((n // 2 + 2, group, LANES), jnp.float32),
             dma((9,)),
             dma((n,)), dma((n,)), dma((n,)), dma((n,)),
-            dma((n,)), dma((n,)), dma((n,)), dma((n,)),
+            dma((kvh // 2 + 1,)), dma((kvh // 2 + 1,)),
+            dma((n // 2,)), dma((n // 2,)), dma((n // 2,)), dma((n // 2,)),
             dma((2,)), dma((2,)),
         ],
         compiler_params=pltpu.CompilerParams(

time: 27.9 us -> 25.4 us (0.910)
  the two profiles are of different devices: /device:TPU:25 before, /device:TPU:0 now
where the time goes in v3:
time: 25.4 us; the launch traced here: 25.2 us
  Pallas kernels  23.8 us (94%)
  local copies, waits for them, and re-layouts  1.36 us (5%)
    pallas_call x1, Pallas kernels, per_device(): pl.pallas_call(functools.partial(kernel, n, kvh, group), out_shape=jax.Sh...  23.8 us
    unnamed x1, local copies, waits for them, and re-layouts  1.36 us

profile of v3, /device:TPU:0, one launch (start us, length us, event | category | flops | bytes accessed | tf_op | source)
XLA Modules:
  0.0 25.2 jit_solution(1196270997158103161)
XLA Ops:
  0.0 23.8 %shard_map.91 = bf16[64,128]{1,0:T(8,128)(2,1)} custom-call(s32[8]{0:T(128)} %len_hbm.1, bf16[1,8192]{1,0:T(2,128)(2,1)} %q_hbm.1, bf16[1,1024]{1,0:T(2,128)(2,1)} %nk_hbm.1, bf16[1,1024]{1,0:T(2,128)(2,1)} %nv_hbm.1, s32[1,32]{1,0:T(1,128)} %keep_hbm.1, bf16[1024,1024]{1,0:T(8,128)(2,1)} %dk_hbm.1, bf16[1024,1024]{1,0:T(8,128)(2,1)} %dv_hbm.1, ...), custom_call_target="tpu_custom_call" | custom-call | tf_op jit(solution)/shard_map/pallas_call | solution.py:357
  23.8 1.4 %copy.12 = bf16[1,1,64,128]{3,1,2,0:T(2,128)(2,1)} copy(bf16[1,1,64,128]{3,2,1,0:T(8,128)(2,1)} %bitcast.5) | data formatting | bytes 32768

commit v4 on v3

--- a/solution.py
+++ b/solution.py
@@ -43,7 +43,7 @@
     len_ref, q_ref, nk_ref, nv_ref, keep_ref,
     dk, dv, sk, sv, q_rows, q_all, lists, bias_ref, units, stats, mate_units, mate_stats, merged, merged_stats, suf_units, suf_stats,
     in_units, in_stats,
-    load_sem, q_send, q_recv, l_send, l_recv, m_send, m_recv, u_send, u_recv, s_send, s_recv, p_send, p_recv,
+    load_sem, q_send, q_recv, l_send, l_recv, m_send, m_recv, t_send, t_recv, u_send, u_recv, s_send, s_recv, p_send, p_recv,
 ):
     part = lax.axis_index("parts")
     me = lax.axis_index("seq")
@@ -58,6 +58,15 @@
     def peer_of(i):
         return lax.rem(me + 2 * i, n)
 
+    barrier = pltpu.get_barrier_semaphore()
+    pl.semaphore_signal(barrier, inc=1, device_id=(part, partner), device_id_type=MESH)
+
+    def greet(i, carry):
+        pl.semaphore_signal(barrier, inc=1, device_id=(part, peer_of(i)), device_id_type=MESH)
+        return carry
+
+    lax.fori_loop(1, chips, greet, 0)
+
     loads = []
     pairs = (
         (q_hbm, q_ref), (keep_hbm, keep_ref), (len_hbm, len_ref), (nk_hbm, nk_ref), (nv_hbm, nv_ref),
@@ -67,15 +76,6 @@
         load = pltpu.make_async_copy(source, target, load_sem.at[index])
         load.start()
         loads.append(load)
-
-    barrier = pltpu.get_barrier_semaphore()
-    pl.semaphore_signal(barrier, inc=1, device_id=(part, partner), device_id_type=MESH)
-
-    def greet(i, carry):
-        pl.semaphore_signal(barrier, inc=1, device_id=(part, peer_of(i)), device_id_type=MESH)
-        return carry
-
-    lax.fori_loop(1, chips, greet, 0)
 
     loads[0].wait()
     for h in range(heads):
@@ -115,11 +115,19 @@
             device_id=(part, partner), device_id_type=MESH,
         )
 
-    def mate_stats_copy():
-        return pltpu.make_async_remote_copy(
-            src_ref=stats.at[1 - parity], dst_ref=mate_stats,
-            send_sem=m_send.at[kvh // 2], recv_sem=m_recv.at[kvh // 2],
+    def mate_stats_copy(pair):
+        return pltpu.make_async_remote_copy(
+            src_ref=stats.at[pair, 1 - parity], dst_ref=mate_stats.at[pair],
+            send_sem=t_send.at[pair], recv_sem=t_recv.at[pair],
             device_id=(part, partner), device_id_type=MESH,
+        )
+
+    def u_piece(device, target, pair):
+        rows = slice(2 * group * pair, 2 * group * (pair + 1))
+        return pltpu.make_async_remote_copy(
+            src_ref=merged.at[device // 2, rows, :], dst_ref=in_units.at[target, rows, :],
+            send_sem=u_send.at[device // 2], recv_sem=u_recv.at[target],
+            device_id=(part, device), device_id_type=MESH,
         )
 
     def u_copy(device, target):
@@ -219,71 +227,68 @@
     loads[8].wait()
     chunk = min(n, TOKENS)
 
-    def span(start):
+    def over_chunks(work):
+        if n > chunk:
+            def step(c, carry):
+                work(c * chunk)
+                return carry
+
+            lax.fori_loop(0, n // chunk, step, 0)
+        else:
+            work(0)
+
+    def mask(start):
         both = lists[pl.ds(start, chunk)].reshape(chunk // 2, 2, 1, width)
         both = jnp.maximum(both[:, 0], both[:, 1])
         for b in range(blocks):
             hit = jnp.max(jnp.where(both == me * blocks + b, 0.0, DEAD), axis=-1, keepdims=True)
-            bias_ref[:, :, b * BLOCK : (b + 1) * BLOCK] = jnp.broadcast_to(hit, (chunk // 2, 8, BLOCK))
+            bias_ref[pl.ds(start // 2, chunk // 2), :, b * BLOCK : (b + 1) * BLOCK] = jnp.broadcast_to(hit, (chunk // 2, 8, BLOCK))
+
+    def span(pair, start):
+        rows = slice(2 * group * pair, 2 * group * (pair + 1))
+        q_pair = q_all[pl.ds(start, chunk), rows, :].astype(jnp.float32)
         stat = jnp.zeros((chunk, group, LANES), jnp.float32)
-        for pair in range(kvh // 2):
-            q_pair = q_all[pl.ds(start, chunk), 2 * group * pair : 2 * group * (pair + 1), :].astype(jnp.float32)
-            made = []
-            for half in range(2):
-                h = 2 * pair + half
-                cols = slice(h * HD, (h + 1) * HD)
-                q_head = q_pair[:, half * group : (half + 1) * group, :]
-                scores = lax.dot_general(
-                    q_head.reshape(chunk * group, HD).astype(jnp.bfloat16), dk[:, cols], NT,
-                    preferred_element_type=jnp.float32,
-                ).reshape(chunk, group, keys)
-                bias = jnp.broadcast_to(
-                    bias_ref[...][:, None], (chunk // 2, 2, group, keys)
-                ).reshape(chunk, group, keys)
-                top, total, out = softmax_terms(scores, bias, dv[:, cols])
-                made.append(out * (1.0 / jnp.maximum(total, 1.0)))
-                stat = jnp.where(lane == h, top, stat)
-                stat = jnp.where(lane == kvh + h, total, stat)
-            unit = jnp.concatenate(made, axis=1).astype(jnp.bfloat16).reshape(chunk // 2, 2, 2 * group, HD)
-            for side in range(2):
-                units[side, pl.ds(start // 2, chunk // 2), 2 * group * pair : 2 * group * (pair + 1), :] = unit[:, side]
-            if n == chunk:
-                mate_copy(pair).start()
+        made = []
+        for half in range(2):
+            h = 2 * pair + half
+            cols = slice(h * HD, (h + 1) * HD)
+            q_head = q_pair[:, half * group : (half + 1) * group, :]
+            scores = lax.dot_general(
+                q_head.reshape(chunk * group, HD).astype(jnp.bfloat16), dk[:, cols], NT,
+                preferred_element_type=jnp.float32,
+            ).reshape(chunk, group, keys)
+            bias = jnp.broadcast_to(
+                bias_ref[pl.ds(start // 2, chunk // 2)][:, None], (chunk // 2, 2, group, keys)
+            ).reshape(chunk, group, keys)
+            top, total, out = softmax_terms(scores, bias, dv[:, cols])
+            made.append(out * (1.0 / jnp.maximum(total, 1.0)))
+            stat = jnp.where(lane == h, top, stat)
+            stat = jnp.where(lane == kvh + h, total, stat)
+        unit = jnp.concatenate(made, axis=1).astype(jnp.bfloat16).reshape(chunk // 2, 2, 2 * group, HD)
         stat = stat.reshape(chunk // 2, 2, group, LANES)
         for side in range(2):
-            stats[side, pl.ds(start // 2, chunk // 2)] = stat[:, side]
-
-    if n > chunk:
-        def step(c, carry):
-            span(c * chunk)
-            return carry
-
-        lax.fori_loop(0, n // chunk, step, 0)
-        for pair in range(kvh // 2):
-            mate_copy(pair).start()
-    else:
-        span(0)
-
-    mate_stats_copy().start()
-
-    mate_stats_copy().wait()
-    mine, other = stats[parity], mate_stats[...]
+            units[side, pl.ds(start // 2, chunk // 2), rows, :] = unit[:, side]
+            stats[pair, side, pl.ds(start // 2, chunk // 2)] = stat[:, side]
 
     def aligned(values):
         return pltpu.roll(values.reshape(-1, LANES), LANES - kvh, 1).reshape(values.shape)
 
-    joint = jnp.maximum(mine, other)
-    mine_part = jnp.exp2((mine - joint) * COEF) * aligned(mine)
-    other_part = jnp.exp2((other - joint) * COEF) * aligned(other)
-    total = mine_part + other_part
-    shares = 1.0 / jnp.maximum(total, 1.0)
-    mine_part = mine_part * shares
-    other_part = other_part * shares
-    shifted = pltpu.roll(total.reshape(-1, LANES), kvh, 1).reshape(total.shape)
-    merged_stats[...] = jnp.where(lane < kvh, joint, shifted)
-    for pair in range(kvh // 2):
+    def merge(pair):
         rows = slice(2 * group * pair, 2 * group * (pair + 1))
+        mate_stats_copy(pair).wait()
         mate_copy(pair).wait()
+        mine, other = stats[pair, parity], mate_stats[pair]
+        joint = jnp.maximum(mine, other)
+        mine_part = jnp.exp2((mine - joint) * COEF) * aligned(mine)
+        other_part = jnp.exp2((other - joint) * COEF) * aligned(other)
+        total = mine_part + other_part
+        shares = 1.0 / jnp.maximum(total, 1.0)
+        mine_part = mine_part * shares
+        other_part = other_part * shares
+        shifted = pltpu.roll(total.reshape(-1, LANES), kvh, 1).reshape(total.shape)
+        fresh = jnp.where(lane < kvh, joint, shifted)
+        fresh = jnp.where(lax.rem(lane, kvh) // 2 == pair, fresh, 0.0)
+        merged_stats[...] = fresh if pair == 0 else merged_stats[...] + fresh
         first = units[parity, :, rows, :].astype(jnp.float32)
         second = mate_units[:, rows, :].astype(jnp.float32)
         made = []
@@ -296,9 +301,24 @@
             )
         merged[:, rows, :] = jnp.concatenate(made, axis=1).astype(jnp.bfloat16)
 
+        def deliver_piece(i, carry):
+            u_piece(peer_of(i), row, pair).start()
+            return carry
+
+        lax.fori_loop(1, chips, deliver_piece, 0)
+
+    over_chunks(mask)
+    pairs_here = kvh // 2
+    for pair in range(pairs_here):
+        over_chunks(functools.partial(span, pair))
+        mate_stats_copy(pair).start()
+        mate_copy(pair).start()
+        if pair > 0:
+            merge(pair - 1)
+    merge(pairs_here - 1)
+
     def deliver(i, carry):
         s_copy(peer_of(i), row).start()
-        u_copy(peer_of(i), row).start()
         return carry
 
     lax.fori_loop(1, chips, deliver, 0)
@@ -372,11 +392,11 @@
             pltpu.VMEM((heads, HD), jnp.float32),
             pltpu.VMEM((n, heads, HD), jnp.bfloat16),
             pltpu.VMEM((n, 1, width), jnp.int32),
-            pltpu.VMEM((min(n, TOKENS) // 2, 8, keys), jnp.float32),
+            pltpu.VMEM((n // 2, 8, keys), jnp.float32),
             pltpu.VMEM((2, n // 2, heads, HD), jnp.bfloat16),
-            pltpu.VMEM((2, n // 2, group, LANES), jnp.float32),
+            pltpu.VMEM((kvh // 2, 2, n // 2, group, LANES), jnp.float32),
             pltpu.VMEM((n // 2, heads, HD), jnp.bfloat16),
-            pltpu.VMEM((n // 2, group, LANES), jnp.float32),
+            pltpu.VMEM((kvh // 2, n // 2, group, LANES), jnp.float32),
             pltpu.VMEM((n // 2, heads, HD), jnp.bfloat16),
             pltpu.VMEM((n // 2, group, LANES), jnp.float32),
             pltpu.VMEM((2, heads, HD), jnp.bfloat16),
@@ -385,7 +405,7 @@
             pltpu.VMEM((n // 2 + 2, group, LANES), jnp.float32),
             dma((9,)),
             dma((n,)), dma((n,)), dma((n,)), dma((n,)),
-            dma((kvh // 2 + 1,)), dma((kvh // 2 + 1,)),
+            dma((kvh // 2,)), dma((kvh // 2,)), dma((kvh // 2,)), dma((kvh // 2,)),
             dma((n // 2,)), dma((n // 2,)), dma((n // 2,)), dma((n // 2,)),
             dma((2,)), dma((2,)),
         ],

time: 25.4 us -> 25.7 us (1.012)
  Pallas kernels: 23.8 us -> 24.1 us
    pallas_call x1, Pallas kernels: 23.8 us -> 24.1 us  [per_device(): pl.pallas_call(functools.partial(kernel, n, kvh, group), out_shape=jax.Sh...]
where the time goes in v4:
time: 25.7 us; the launch traced here: 25.5 us
  Pallas kernels  24.1 us (94%)
  local copies, waits for them, and re-layouts  1.36 us (5%)
    pallas_call x1, Pallas kernels, per_device(): pl.pallas_call(functools.partial(kernel, n, kvh, group), out_shape=jax.Sh...  24.1 us
    unnamed x1, local copies, waits for them, and re-layouts  1.36 us

profile of v4, /device:TPU:0, one launch (start us, length us, event | category | flops | bytes accessed | tf_op | source)
XLA Modules:
  0.0 25.5 jit_solution(6566175842778679765)
XLA Ops:
  0.0 24.1 %shard_map.91 = bf16[64,128]{1,0:T(8,128)(2,1)} custom-call(s32[8]{0:T(128)} %len_hbm.1, bf16[1,8192]{1,0:T(2,128)(2,1)} %q_hbm.1, bf16[1,1024]{1,0:T(2,128)(2,1)} %nk_hbm.1, bf16[1,1024]{1,0:T(2,128)(2,1)} %nv_hbm.1, s32[1,32]{1,0:T(1,128)} %keep_hbm.1, bf16[1024,1024]{1,0:T(8,128)(2,1)} %dk_hbm.1, bf16[1024,1024]{1,0:T(8,128)(2,1)} %dv_hbm.1, ...), custom_call_target="tpu_custom_call" | custom-call | tf_op jit(solution)/shard_map/pallas_call | solution.py:377
  24.1 1.4 %copy.12 = bf16[1,1,64,128]{3,1,2,0:T(2,128)(2,1)} copy(bf16[1,1,64,128]{3,2,1,0:T(8,128)(2,1)} %bitcast.5) | data formatting | bytes 32768

commit v5 on v4

--- a/solution.py
+++ b/solution.py
@@ -58,6 +58,13 @@
     def peer_of(i):
         return lax.rem(me + 2 * i, n)
 
+    def each_chip(work):
+        if chips <= TOKENS:
+            for i in range(1, chips):
+                work(i, 0)
+        else:
+            lax.fori_loop(1, chips, work, 0)
+
     barrier = pltpu.get_barrier_semaphore()
     pl.semaphore_signal(barrier, inc=1, device_id=(part, partner), device_id_type=MESH)
 
@@ -65,7 +72,7 @@
         pl.semaphore_signal(barrier, inc=1, device_id=(part, peer_of(i)), device_id_type=MESH)
         return carry
 
-    lax.fori_loop(1, chips, greet, 0)
+    each_chip(greet)
 
     loads = []
     pairs = (
@@ -123,7 +130,7 @@
         )
 
     def u_piece(device, target, pair):
-        rows = slice(2 * group * pair, 2 * group * (pair + 1))
+        rows = slice(2 * group * (pair - 1), 2 * group * (pair + 1))
         return pltpu.make_async_remote_copy(
             src_ref=merged.at[device // 2, rows, :], dst_ref=in_units.at[target, rows, :],
             send_sem=u_send.at[device // 2], recv_sem=u_recv.at[target],
@@ -152,7 +159,7 @@
         l_copy(peer_of(i), me, peer_of(i)).start()
         return carry
 
-    lax.fori_loop(1, chips, share, 0)
+    each_chip(share)
 
     loads[2].wait()
     loads[3].wait()
@@ -215,14 +222,14 @@
         l_copy(partner, slot, slot + flip).start()
         return carry
 
-    lax.fori_loop(1, chips, forward, 0)
+    each_chip(forward)
 
     def arrive(i, carry):
         q_copy(partner, peer_of(i) + flip, me).wait_recv()
         l_copy(partner, peer_of(i) + flip, me).wait_recv()
         return carry
 
-    lax.fori_loop(1, chips, arrive, 0)
+    each_chip(arrive)
     loads[7].wait()
     loads[8].wait()
     chunk = min(n, TOKENS)
@@ -305,7 +312,8 @@
             u_piece(peer_of(i), row, pair).start()
             return carry
 
-        lax.fori_loop(1, chips, deliver_piece, 0)
+        if pair % 2 == 1:
+            each_chip(deliver_piece)
 
     over_chunks(mask)
     pairs_here = kvh // 2
@@ -321,7 +329,7 @@
         s_copy(peer_of(i), row).start()
         return carry
 
-    lax.fori_loop(1, chips, deliver, 0)
+    each_chip(deliver)
     in_units[row] = merged[row]
     in_stats[row] = merged_stats[row]
     q_copy(partner, me, partner).wait_send()
@@ -334,7 +342,7 @@
         l_copy(partner, peer_of(i), peer_of(i) + flip).wait_send()
         return carry
 
-    lax.fori_loop(1, chips, q_sent, 0)
+    each_chip(q_sent)
     for copy in suffix_copies:
         copy.wait()
 
@@ -343,7 +351,7 @@
         u_copy(peer_of(i), peer_of(i) // 2).wait_recv()
         return carry
 
-    lax.fori_loop(1, chips, collect, 0)
+    each_chip(collect)
 
     tops = in_stats[...]
     ceiling = jnp.max(tops, axis=0, keepdims=True)
@@ -363,7 +371,7 @@
         u_copy(peer_of(i), row).wait_send()
         return carry
 
-    lax.fori_loop(1, chips, u_sent, 0)
+    each_chip(u_sent)
 
 
 def per_device(n, queries, new_keys, new_values, doc_keys, doc_values, suffix_keys, suffix_values, keep_lists, suffix_lengths):

time: 25.7 us -> 25.8 us (level)
  no operation moved by 1% of the time
where the time goes in v5:
time: 25.8 us; the launch traced here: 25.6 us
  Pallas kernels  24.2 us (94%)
  local copies, waits for them, and re-layouts  1.36 us (5%)
    pallas_call x1, Pallas kernels, per_device(): pl.pallas_call(functools.partial(kernel, n, kvh, group), out_shape=jax.Sh...  24.2 us
    unnamed x1, local copies, waits for them, and re-layouts  1.36 us

profile of v5, /device:TPU:0, one launch (start us, length us, event | category | flops | bytes accessed | tf_op | source)
XLA Modules:
  0.0 25.6 jit_solution(15592975604295946845)
XLA Ops:
  0.0 24.2 %shard_map.91 = bf16[64,128]{1,0:T(8,128)(2,1)} custom-call(s32[8]{0:T(128)} %len_hbm.1, bf16[1,8192]{1,0:T(2,128)(2,1)} %q_hbm.1, bf16[1,1024]{1,0:T(2,128)(2,1)} %nk_hbm.1, bf16[1,1024]{1,0:T(2,128)(2,1)} %nv_hbm.1, s32[1,32]{1,0:T(1,128)} %keep_hbm.1, bf16[1024,1024]{1,0:T(8,128)(2,1)} %dk_hbm.1, bf16[1024,1024]{1,0:T(8,128)(2,1)} %dv_hbm.1, ...), custom_call_target="tpu_custom_call" | custom-call | tf_op jit(solution)/shard_map/pallas_call | solution.py:385
  24.2 1.4 %copy.12 = bf16[1,1,64,128]{3,1,2,0:T(2,128)(2,1)} copy(bf16[1,1,64,128]{3,2,1,0:T(8,128)(2,1)} %bitcast.5) | data formatting | bytes 32768

commit v6 on v3

--- a/solution.py
+++ b/solution.py
@@ -11,6 +11,7 @@
 HD = 128
 BLOCK = 128
 LANES = 128
+ID_ROWS = 16
 TOKENS = 16
 
 DEAD = -1e30
@@ -41,9 +42,9 @@
     len_hbm, q_hbm, nk_hbm, nv_hbm, keep_hbm, dk_hbm, dv_hbm, sk_hbm, sv_hbm,
     out_ref,
     len_ref, q_ref, nk_ref, nv_ref, keep_ref,
-    dk, dv, sk, sv, q_rows, q_all, lists, bias_ref, units, stats, mate_units, mate_stats, merged, merged_stats, suf_units, suf_stats,
+    dk, dv, sk, sv, q_rows, q_all, bias_ref, units, stats, mate_units, mate_stats, merged, merged_stats, suf_units, suf_stats,
     in_units, in_stats,
-    load_sem, q_send, q_recv, l_send, l_recv, m_send, m_recv, u_send, u_recv, s_send, s_recv, p_send, p_recv,
+    load_sem, q_send, q_recv, m_send, m_recv, u_send, u_recv, s_send, s_recv, p_send, p_recv,
 ):
     part = lax.axis_index("parts")
     me = lax.axis_index("seq")
@@ -58,6 +59,15 @@
     def peer_of(i):
         return lax.rem(me + 2 * i, n)
 
+    barrier = pltpu.get_barrier_semaphore()
+    pl.semaphore_signal(barrier, inc=1, device_id=(part, partner), device_id_type=MESH)
+
+    def greet(i, carry):
+        pl.semaphore_signal(barrier, inc=1, device_id=(part, peer_of(i)), device_id_type=MESH)
+        return carry
+
+    lax.fori_loop(1, chips, greet, 0)
+
     loads = []
     pairs = (
         (q_hbm, q_ref), (keep_hbm, keep_ref), (len_hbm, len_ref), (nk_hbm, nk_ref), (nv_hbm, nv_ref),
@@ -68,28 +78,26 @@
         load.start()
         loads.append(load)
 
-    barrier = pltpu.get_barrier_semaphore()
-    pl.semaphore_signal(barrier, inc=1, device_id=(part, partner), device_id_type=MESH)
-
-    def greet(i, carry):
-        pl.semaphore_signal(barrier, inc=1, device_id=(part, peer_of(i)), device_id_type=MESH)
-        return carry
-
-    lax.fori_loop(1, chips, greet, 0)
-
     loads[0].wait()
     for h in range(heads):
         q_rows[h : h + 1, :] = q_ref[0:1, h * HD : (h + 1) * HD].astype(jnp.float32)
-    q_all[me] = q_rows[...].astype(jnp.bfloat16)
     kept = keep_ref.shape[1]
-    width = lists.shape[2]
+    width = -(-2 * kept // LANES) * LANES
     loads[1].wait()
     ids = keep_ref[...]
     blank = jnp.full((1, kept), -1, jnp.int32)
     pieces = [jnp.where(parity == 0, ids, blank), jnp.where(parity == 1, ids, blank)]
     if width > 2 * kept:
         pieces.append(jnp.full((1, width - 2 * kept), -1, jnp.int32))
-    lists[me] = jnp.concatenate(pieces, axis=1)
+    ids = jnp.concatenate(pieces, axis=1)
+    q_rows[heads:, :] = jnp.zeros((ID_ROWS, LANES), jnp.float32)
+    for w in range(width // LANES):
+        piece = ids[:, w * LANES : (w + 1) * LANES]
+        low = heads + w
+        high = heads + ID_ROWS // 2 + w
+        q_rows[low : low + 1, :] = (piece & 255).astype(jnp.float32)
+        q_rows[high : high + 1, :] = (piece >> 8).astype(jnp.float32)
+    q_all[me] = q_rows[...].astype(jnp.bfloat16)
 
     pl.semaphore_wait(barrier, chips)
 
@@ -97,13 +105,6 @@
         return pltpu.make_async_remote_copy(
             src_ref=q_all.at[slot], dst_ref=q_all.at[slot],
             send_sem=q_send.at[send], recv_sem=q_recv.at[slot],
-            device_id=(part, device), device_id_type=MESH,
-        )
-
-    def l_copy(device, slot, send):
-        return pltpu.make_async_remote_copy(
-            src_ref=lists.at[slot], dst_ref=lists.at[slot],
-            send_sem=l_send.at[send], recv_sem=l_recv.at[slot],
             device_id=(part, device), device_id_type=MESH,
         )
 
@@ -137,11 +138,9 @@
         )
 
     q_copy(partner, me, partner).start()
-    l_copy(partner, me, partner).start()
 
     def share(i, carry):
         q_copy(peer_of(i), me, peer_of(i)).start()
-        l_copy(peer_of(i), me, peer_of(i)).start()
         return carry
 
     lax.fori_loop(1, chips, share, 0)
@@ -196,22 +195,18 @@
     for copy in suffix_copies:
         copy.start()
 
-    l_copy(partner, partner, me).wait_recv()
     flip = 1 - 2 * parity
 
     def forward(i, carry):
         slot = peer_of(i)
         q_copy(partner, slot, slot + flip).wait_recv()
         q_copy(partner, slot, slot + flip).start()
-        l_copy(partner, slot, slot + flip).wait_recv()
-        l_copy(partner, slot, slot + flip).start()
         return carry
 
     lax.fori_loop(1, chips, forward, 0)
 
     def arrive(i, carry):
         q_copy(partner, peer_of(i) + flip, me).wait_recv()
-        l_copy(partner, peer_of(i) + flip, me).wait_recv()
         return carry
 
     lax.fori_loop(1, chips, arrive, 0)
@@ -220,10 +215,15 @@
     chunk = min(n, TOKENS)
 
     def span(start):
-        both = lists[pl.ds(start, chunk)].reshape(chunk // 2, 2, 1, width)
+        tail = q_all[pl.ds(start, chunk), heads:, :].astype(jnp.float32)
+        both = [
+            tail[:, w : w + 1, :] + 256.0 * tail[:, ID_ROWS // 2 + w : ID_ROWS // 2 + w + 1, :]
+            for w in range(width // LANES)
+        ]
+        both = jnp.concatenate(both, axis=-1).reshape(chunk // 2, 2, 1, width)
         both = jnp.maximum(both[:, 0], both[:, 1])
         for b in range(blocks):
-            hit = jnp.max(jnp.where(both == me * blocks + b, 0.0, DEAD), axis=-1, keepdims=True)
+            hit = jnp.max(jnp.where(both == (me * blocks + b).astype(jnp.float32), 0.0, DEAD), axis=-1, keepdims=True)
             bias_ref[:, :, b * BLOCK : (b + 1) * BLOCK] = jnp.broadcast_to(hit, (chunk // 2, 8, BLOCK))
         stat = jnp.zeros((chunk, group, LANES), jnp.float32)
         for pair in range(kvh // 2):
@@ -305,13 +305,10 @@
     in_units[row] = merged[row]
     in_stats[row] = merged_stats[row]
     q_copy(partner, me, partner).wait_send()
-    l_copy(partner, me, partner).wait_send()
 
     def q_sent(i, carry):
         q_copy(peer_of(i), me, peer_of(i)).wait_send()
-        l_copy(peer_of(i), me, peer_of(i)).wait_send()
         q_copy(partner, peer_of(i), peer_of(i) + flip).wait_send()
-        l_copy(partner, peer_of(i), peer_of(i) + flip).wait_send()
         return carry
 
     lax.fori_loop(1, chips, q_sent, 0)
@@ -350,7 +347,6 @@
     heads = queries.shape[1] // HD
     kvh = new_keys.shape[1] // HD
     group = heads // kvh
-    width = -(-2 * keep_lists.shape[1] // LANES) * LANES
     keys, columns = doc_keys.shape
     hbm = pl.BlockSpec(memory_space=pltpu.HBM)
     dma = pltpu.SemaphoreType.DMA
@@ -369,9 +365,8 @@
             pltpu.VMEM((keys, columns), jnp.bfloat16),
             pltpu.VMEM(suffix_keys.shape, jnp.bfloat16),
             pltpu.VMEM(suffix_keys.shape, jnp.bfloat16),
-            pltpu.VMEM((heads, HD), jnp.float32),
-            pltpu.VMEM((n, heads, HD), jnp.bfloat16),
-            pltpu.VMEM((n, 1, width), jnp.int32),
+            pltpu.VMEM((heads + ID_ROWS, HD), jnp.float32),
+            pltpu.VMEM((n, heads + ID_ROWS, HD), jnp.bfloat16),
             pltpu.VMEM((min(n, TOKENS) // 2, 8, keys), jnp.float32),
             pltpu.VMEM((2, n // 2, heads, HD), jnp.bfloat16),
             pltpu.VMEM((2, n // 2, group, LANES), jnp.float32),
@@ -384,7 +379,7 @@
             pltpu.VMEM((n // 2 + 2, heads, HD), jnp.bfloat16),
             pltpu.VMEM((n // 2 + 2, group, LANES), jnp.float32),
             dma((9,)),
-            dma((n,)), dma((n,)), dma((n,)), dma((n,)),
+            dma((n,)), dma((n,)),
             dma((kvh // 2 + 1,)), dma((kvh // 2 + 1,)),
             dma((n // 2,)), dma((n // 2,)), dma((n // 2,)), dma((n // 2,)),
             dma((2,)), dma((2,)),

time: 25.4 us -> 25.5 us (level)
  no operation moved by 1% of the time
where the time goes in v6:
time: 25.5 us; the launch traced here: 25.3 us
  Pallas kernels  23.9 us (94%)
  local copies, waits for them, and re-layouts  1.36 us (5%)
    pallas_call x1, Pallas kernels, per_device(): pl.pallas_call(functools.partial(kernel, n, kvh, group), out_shape=jax.Sh...  23.9 us
    unnamed x1, local copies, waits for them, and re-layouts  1.36 us

profile of v6, /device:TPU:0, one launch (start us, length us, event | category | flops | bytes accessed | tf_op | source)
XLA Modules:
  0.0 25.3 jit_solution(13811386852798677106)
XLA Ops:
  0.0 23.9 %shard_map.91 = bf16[64,128]{1,0:T(8,128)(2,1)} custom-call(s32[8]{0:T(128)} %len_hbm.1, bf16[1,8192]{1,0:T(2,128)(2,1)} %q_hbm.1, bf16[1,1024]{1,0:T(2,128)(2,1)} %nk_hbm.1, bf16[1,1024]{1,0:T(2,128)(2,1)} %nv_hbm.1, s32[1,32]{1,0:T(1,128)} %keep_hbm.1, bf16[1024,1024]{1,0:T(8,128)(2,1)} %dk_hbm.1, bf16[1024,1024]{1,0:T(8,128)(2,1)} %dv_hbm.1, ...), custom_call_target="tpu_custom_call" | custom-call | tf_op jit(solution)/shard_map/pallas_call | solution.py:353
  23.9 1.4 %copy.12 = bf16[1,1,64,128]{3,1,2,0:T(2,128)(2,1)} copy(bf16[1,1,64,128]{3,2,1,0:T(8,128)(2,1)} %bitcast.5) | data formatting | bytes 32768
